TPU v7x, 256 devices: a whole 4x4x8 slice. The times are simulated.
256 devices in a mesh: lon: 16 (over y_lo, z), lat: 16 (over x, y_hi, core).
Axes of the slice: x: 4, y: 4 (y_hi: 2, y_lo: 2; y = y_hi * 2 + y_lo), z: 8, core: 2. Of those that a mesh axis runs over, the one named last changes fastest.
Arguments:
- tracers: float32 [4, 8, 256, 2048], P(None, None, 'lat', 'lon'), may hold values from -6 to 6
- courant_frac: float32 [8, 256, 2048], P(None, 'lat', 'lon'), may hold values from 0 to 1
- shifts: int32 [8, 256], P(None, 'lat'), may hold values from -384 to 383
- merid: float32 [8, 256, 2048], P(None, 'lat', 'lon'), may hold values from -0.9 to 0.9
Outputs:
- updated: float32 [4, 8, 256, 2048], P(None, None, 'lat', 'lon')
- zonal_flux: float32 [4, 8, 256, 2048], P(None, None, 'lat', 'lon')
All inputs are finite; a program needn't handle non-finite values.
Results may differ from a plain program's by a relative error of at most 0.0003.
Values sent between devices are 32-bit elements; how exact they have to be, the bound alone decides.
A program may use at most 64 MiB of HBM per device.

v0:
```python
import jax
import jax.numpy as jnp
from jax import lax
from jax.sharding import PartitionSpec as P

REACH = 3


def extended(block, sides, width, periodic):
    for axis, dim in sides:
        count = lax.axis_size(axis)
        forward = [(i, i + 1) for i in range(count - 1)]
        if periodic:
            forward.append((count - 1, 0))
        backward = [(target, source) for source, target in forward]
        low = lax.ppermute(
            lax.slice_in_dim(block, block.shape[dim] - width, None, axis=dim), axis, forward
        )
        high = lax.ppermute(lax.slice_in_dim(block, 0, width, axis=dim), axis, backward)
        block = jnp.concatenate([low, block, high], axis=dim)
    return block


def passed_along(array, axis, by):
    size = lax.axis_size(axis)
    return lax.ppermute(array, axis, [(i, (i + by) % size) for i in range(size)])


def cell_part(values, slopes, weight):
    return values * weight + slopes * (weight * weight - weight) * 0.5


def align_window(stacked, remain, lon_count):
    current = stacked
    for bit in range((lon_count - 1).bit_length()):
        step = 1 << bit
        moved = jnp.concatenate((current[..., step:], jnp.zeros_like(current[..., :step])), axis=-1)
        flag = (jnp.bitwise_and(remain, step) != 0)[None, None, :, :, None]
        current = jnp.where(flag, moved, current)
    return current


def per_device(tracers, courant_frac, shifts, merid):
    tracer_count = tracers.shape[0]
    row_count = tracers.shape[2]
    lon_count = tracers.shape[3]
    stacked = jnp.concatenate((tracers, courant_frac[None]), axis=0)
    rimmed = extended(stacked, (("lon", 3),), 1, True)
    slopes = 0.5 * (rimmed[:tracer_count, :, :, 2:] - rimmed[:tracer_count, :, :, :-2])
    frac_west = rimmed[tracer_count, :, :, :lon_count]
    totals = jnp.sum(tracers, axis=3)
    start_cell = -1 - shifts
    low_block = jnp.floor_divide(start_cell, lon_count)
    remain = start_cell - low_block * lon_count
    outgoing = (tracers, slopes, totals)
    arrived = {}
    eastward = outgoing
    westward = outgoing
    for distance in range(1, REACH + 1):
        eastward = passed_along((eastward[0], eastward[1], eastward[2]), "lon", 1)
        westward = passed_along((westward[0], westward[1], westward[2]), "lon", -1)
        arrived[-distance] = eastward
        arrived[distance] = westward

    def blocks_at(offset):
        if offset == 0:
            return (tracers, slopes)
        values = arrived[offset][0]
        sides = arrived[offset][1]
        return (values, sides)

    low_q = jnp.zeros_like(tracers)
    low_s = jnp.zeros_like(tracers)
    high_q = jnp.zeros_like(tracers)
    high_s = jnp.zeros_like(tracers)
    for offset in range(-REACH, REACH + 1):
        values, sides = blocks_at(offset)
        pick_low = (low_block == offset)[None, :, :, None]
        pick_high = (low_block + 1 == offset)[None, :, :, None]
        low_q = jnp.where(pick_low, values, low_q)
        low_s = jnp.where(pick_low, sides, low_s)
        high_q = jnp.where(pick_high, values, high_q)
        high_s = jnp.where(pick_high, sides, high_s)
    offset_sum = jnp.zeros_like(totals)
    running = jnp.zeros_like(totals)
    for distance in range(1, REACH + 1):
        running = running + arrived[-distance][2]
        offset_sum = jnp.where((low_block == -distance)[None], -running, offset_sum)
    running = jnp.zeros_like(totals)
    for distance in range(REACH - 1):
        block_sum = totals if distance == 0 else arrived[distance][2]
        running = running + block_sum
        offset_sum = jnp.where((low_block == distance + 1)[None], running, offset_sum)
    window_q = jnp.concatenate((low_q, high_q), axis=3)
    window_s = jnp.concatenate((low_s, high_s), axis=3)
    window_pre = jnp.cumsum(window_q, axis=3) - window_q
    aligned = align_window(jnp.stack((window_pre, window_q, window_s), axis=0), remain, lon_count)
    west_cells = aligned[..., :lon_count]
    east_cells = aligned[..., 1 : lon_count + 1]
    own_incl = jnp.cumsum(tracers, axis=3)
    own_excl = own_incl - tracers
    weight_east = 1.0 - courant_frac
    weight_west = 1.0 - frac_west
    flux_east = (
        own_incl
        - (offset_sum[..., None] + east_cells[0])
        - cell_part(east_cells[1], east_cells[2], weight_east)
    )
    flux_west = (
        own_excl
        - (offset_sum[..., None] + west_cells[0])
        - cell_part(west_cells[1], west_cells[2], weight_west)
    )
    banded = extended(jnp.concatenate((tracers, merid[None]), axis=0), (("lat", 2),), 2, False)
    band_q = banded[:tracer_count]
    band_v = banded[tracer_count]
    side_y = 0.5 * (band_q[:, :, 2:] - band_q[:, :, :-2])
    global_rows = lax.axis_index("lat") * row_count + jnp.arange(-1, row_count + 1, dtype=jnp.int32)
    total_rows = row_count * lax.axis_size("lat")
    side_y = jnp.where(
        ((global_rows == 0) | (global_rows == total_rows - 1))[None, None, :, None], 0.0, side_y
    )
    face_rows = global_rows[: row_count + 1]
    north_v = jnp.where(
        (face_rows == total_rows - 1)[None, :, None], 0.0, band_v[:, 1 : row_count + 2]
    )
    lower_q = band_q[:, :, 1 : row_count + 2]
    lower_s = side_y[:, :, : row_count + 1]
    upper_q = band_q[:, :, 2 : row_count + 3]
    upper_s = side_y[:, :, 1 : row_count + 2]
    north_flux = jnp.where(
        north_v >= 0.0,
        north_v * lower_q + north_v * (1.0 - north_v) * 0.5 * lower_s,
        north_v * upper_q - north_v * (1.0 + north_v) * 0.5 * upper_s,
    )
    updated = tracers - (flux_east - flux_west) - (north_flux[:, :, 1:] - north_flux[:, :, :-1])
    return (updated, flux_east)


def solution(mesh):
    return jax.shard_map(
        per_device,
        mesh=mesh,
        in_specs=(
            P(None, None, "lat", "lon"),
            P(None, "lat", "lon"),
            P(None, "lat"),
            P(None, "lat", "lon"),
        ),
        out_specs=(P(None, None, "lat", "lon"), P(None, None, "lat", "lon")),
        check_vma=False,
    )
```

profile of v0, /device:TPU:6, one launch (start us, length us, event | category | flops | bytes accessed | tf_op | source)
XLA Modules:
  0.0 120.9 jit_solution(13875604661219331023)
XLA Ops:
  0.7 6.9 %collective-permute-start.4 = (f32[4,8,16,128]{3,2,1,0:T(8,128)}, f32[4,8,16,128]{3,2,1,0:T(8,128)S(1)}, u32[]{:S(2)}, u32[]{:S(2)}) collective-permute-start(f32[4,8,16,128]{3,2,1,0:T(8,128)} %param.4), channel_id=1, source_target_pairs={{0,240},{16,0},{32,16},{48,32},{64,48},{80,64},{96,80},{112,96},{1... | collective-permute-start | bytes 786440 | tf_op jit(solution)/shard_map/ppermute | solution.py:26
  7.6 1.3 %fusion.7 = (f32[5,8,16,1]{3,2,1,0:T(8,128)S(1)}, f32[5,8,16,1]{3,2,1,0:T(8,128)S(1)}) fusion(f32[4,8,16,128]{3,2,1,0:T(8,128)} %param.4, f32[1,8,16,128]{3,2,1,0:T(8,128)} %bitcast.81), kind=kLoop, calls=%fused_computation.28 | loop fusion | flops 1280 | bytes 332800 | tf_op jit(solution)/shard_map/concatenate | solution.py:47
  9.0 4.2 %collective-permute-start.10 = (f32[5,8,16,1]{3,2,1,0:T(8,128)S(1)}, f32[5,8,16,1]{3,2,1,0:T(8,128)S(1)}, u32[]{:S(2)}, u32[]{:S(2)}) collective-permute-start(f32[5,8,16,1]{3,2,1,0:T(8,128)S(1)} %get-tuple-element.13), channel_id=1, source_target_pairs={{16,0},{32,16},{48,32},{64,48},{80,64},{96,80},{112,96},{128,112},... | collective-permute-start | bytes 7688 | tf_op jit(solution)/shard_map/ppermute | solution.py:19
  13.2 1.0 pad_maximum_fusion.11
  14.2 2.1 %collective-permute-start.18 = (f32[5,8,2,128]{3,2,1,0:T(2,128)S(1)}, f32[5,8,2,128]{3,2,1,0:T(2,128)S(1)}, u32[]{:S(2)}, u32[]{:S(2)}) collective-permute-start(f32[5,8,2,128]{3,2,1,0:T(2,128)S(1)} %get-tuple-element.18), channel_id=1, source_target_pairs={{0,1},{1,2},{2,3},{3,4},{4,5},{5,6},{6,7},{7,8},{8,9},{9,10},{10,1... | collective-permute-start | bytes 122888 | tf_op jit(solution)/shard_map/ppermute | solution.py:16
  16.3 1.5 %broadcast_subtract_fusion = (f32[8,16,128]{2,1,0:T(8,128)}, f32[8,16,128]{2,1,0:T(8,128)}) fusion(f32[8,16,128]{2,1,0:T(8,128)} %param.5), kind=kLoop, calls=%fused_computation.84 | loop fusion | flops 49152 | bytes 196608 | tf_op jit(solution)/shard_map/sub | solution.py:102
  17.8 0.6 and_compare_fusion.6
  18.5 0.6 and_compare_fusion.5
  19.1 5.7 %collective-permute-done.11 = f32[5,8,16,1]{3,2,1,0:T(8,128)S(1)} collective-permute-done((f32[5,8,16,1]{3,2,1,0:T(8,128)S(1)}, f32[5,8,16,1]{3,2,1,0:T(8,128)S(1)}, u32[]{:S(2)}, u32[]{:S(2)}) %collective-permute-start.11) | collective-permute-done | bytes 2592 | tf_op jit(solution)/shard_map/ppermute | solution.py:16
  24.8 0.4 fusion.38
  25.3 5.8 %collective-permute-done.1 = f32[4,8,16]{2,1,0:T(8,128)S(1)} collective-permute-done((f32[4,8,16]{2,1,0:T(8,128)S(1)}, f32[4,8,16]{2,1,0:T(8,128)S(1)}, u32[]{:S(2)}, u32[]{:S(2)}) %collective-permute-start.1) | collective-permute-done | bytes 2080 | tf_op jit(solution)/shard_map/ppermute | solution.py:26
  31.1 14.4 %reduce_window_sum.33 = f32[4,8,16,128]{3,2,1,0:T(8,128)} reduce-window(f32[4,8,16,128]{3,2,1,0:T(8,128)S(1)} %copy-done, f32[]{:T(128)} %constant.20.clone.1), window={size=1x1x1x128 pad=0_0x0_0x0_0x127_0}, to_apply=%region_0.0 | reduce-window | flops 8323072 | bytes 524292 | tf_op jit(solution)/shard_map/jit(cumsum)/reduce_window_sum | solution.py:100
  45.5 4.1 %collective-permute-start = (f32[4,8,16]{2,1,0:T(8,128)S(1)}, f32[4,8,16]{2,1,0:T(8,128)S(1)}, u32[]{:S(2)}, u32[]{:S(2)}) collective-permute-start(f32[4,8,16]{2,1,0:T(8,128)S(1)} %get-tuple-element.19), channel_id=1, source_target_pairs={{0,240},{16,0},{32,16},{48,32},{64,48},{80,64},{96,80},{112,96},{1... | collective-permute-start | bytes 6152 | tf_op jit(solution)/shard_map/ppermute | solution.py:26
  49.7 0.7 fusion.29
  50.4 0.7 collective-permute-done
  51.1 1.9 %collective-permute-start.19 = (f32[5,8,2,128]{3,2,1,0:T(2,128)S(1)}, f32[5,8,2,128]{3,2,1,0:T(2,128)S(1)}, u32[]{:S(2)}, u32[]{:S(2)}) collective-permute-start(f32[5,8,2,128]{3,2,1,0:T(2,128)S(1)} %get-tuple-element.17), channel_id=1, source_target_pairs={{1,0},{2,1},{3,2},{4,3},{5,4},{6,5},{7,6},{8,7},{9,8},{10,9},{11,1... | collective-permute-start | bytes 122888 | tf_op jit(solution)/shard_map/ppermute | solution.py:19
  53.0 2.5 %collective-permute-done.3 = f32[4,8,16]{2,1,0:T(8,128)S(1)} collective-permute-done((f32[4,8,16]{2,1,0:T(8,128)S(1)}, f32[4,8,16]{2,1,0:T(8,128)S(1)}, u32[]{:S(2)}, u32[]{:S(2)}) %collective-permute-start.3) | collective-permute-done | bytes 2080 | tf_op jit(solution)/shard_map/ppermute | solution.py:26
  55.5 2.0 %collective-permute-start.12 = (f32[4,8,16,128]{3,2,1,0:T(8,128)S(1)}, f32[4,8,16,128]{3,2,1,0:T(8,128)S(1)}, u32[]{:S(2)}, u32[]{:S(2)}) collective-permute-start(f32[4,8,16,128]{3,2,1,0:T(8,128)S(1)} %get-tuple-element.20), channel_id=1, source_target_pairs={{0,240},{16,0},{32,16},{48,32},{64,48},{80,64},{96,80},{112,96},{1... | collective-permute-start | bytes 786440 | tf_op jit(solution)/shard_map/ppermute | solution.py:26
  57.8 4.2 %collective-permute-start.5 = (f32[4,8,16,128]{3,2,1,0:T(8,128)S(1)}, f32[4,8,16,128]{3,2,1,0:T(8,128)S(1)}, u32[]{:S(2)}, u32[]{:S(2)}) collective-permute-start(f32[4,8,16,128]{3,2,1,0:T(8,128)S(1)} %collective-permute-done.4), channel_id=1, source_target_pairs={{0,240},{16,0},{32,16},{48,32},{64,48},{80,64},{96,80},{112,96},{1... | collective-permute-start | bytes 786440 | tf_op jit(solution)/shard_map/ppermute | solution.py:26
  62.1 0.2 fusion.6
  62.3 1.9 %collective-permute-done.12 = f32[4,8,16,128]{3,2,1,0:T(8,128)S(1)} collective-permute-done((f32[4,8,16,128]{3,2,1,0:T(8,128)S(1)}, f32[4,8,16,128]{3,2,1,0:T(8,128)S(1)}, u32[]{:S(2)}, u32[]{:S(2)}) %collective-permute-start.12) | collective-permute-done | bytes 262176 | tf_op jit(solution)/shard_map/ppermute | solution.py:26
  64.1 4.6 %collective-permute-start.13 = (f32[4,8,16,128]{3,2,1,0:T(8,128)S(1)}, f32[4,8,16,128]{3,2,1,0:T(8,128)}, u32[]{:S(2)}, u32[]{:S(2)}) collective-permute-start(f32[4,8,16,128]{3,2,1,0:T(8,128)S(1)} %collective-permute-done.12), channel_id=1, source_target_pairs={{0,240},{16,0},{32,16},{48,32},{64,48},{80,64},{96,80},{112,96},{1... | collective-permute-start | bytes 786440 | tf_op jit(solution)/shard_map/ppermute | solution.py:26
  68.9 0.9 collective-permute-done.5
  69.7 4.6 %collective-permute-start.6 = (f32[4,8,16,128]{3,2,1,0:T(8,128)S(1)}, f32[4,8,16,128]{3,2,1,0:T(8,128)S(1)}, u32[]{:S(2)}, u32[]{:S(2)}) collective-permute-start(f32[4,8,16,128]{3,2,1,0:T(8,128)S(1)} %collective-permute-done.5), channel_id=1, source_target_pairs={{0,240},{16,0},{32,16},{48,32},{64,48},{80,64},{96,80},{112,96},{1... | collective-permute-start | bytes 786440 | tf_op jit(solution)/shard_map/ppermute | solution.py:26
  74.5 0.2 fusion.3
  74.6 0.8 collective-permute-done.13
  75.5 4.7 %collective-permute-start.14 = (f32[4,8,16,128]{3,2,1,0:T(8,128)}, f32[4,8,16,128]{3,2,1,0:T(8,128)}, u32[]{:S(2)}, u32[]{:S(2)}) collective-permute-start(f32[4,8,16,128]{3,2,1,0:T(8,128)} %collective-permute-done.13), channel_id=1, source_target_pairs={{0,240},{16,0},{32,16},{48,32},{64,48},{80,64},{96,80},{112,96},{1... | collective-permute-start | bytes 786440 | tf_op jit(solution)/shard_map/ppermute | solution.py:26
  80.3 0.8 collective-permute-done.6
  81.1 4.7 %collective-permute-done.9 = f32[4,8,16,128]{3,2,1,0:T(8,128)S(1)} collective-permute-done((f32[4,8,16,128]{3,2,1,0:T(8,128)S(1)}, f32[4,8,16,128]{3,2,1,0:T(8,128)S(1)}, u32[]{:S(2)}, u32[]{:S(2)}) %collective-permute-start.9) | collective-permute-done | bytes 262176 | tf_op jit(solution)/shard_map/ppermute | solution.py:26
  85.9 0.2 select_select_fusion.3
  86.2 0.2 select_select_fusion.2
  86.5 18.1 %reduce-window.6 = f32[4,8,16,2,128]{4,2,3,1,0:T(8,128)S(1)} reduce-window(f32[4,8,16,2,128]{4,2,3,1,0:T(8,128)S(1)} %bitcast.80, f32[]{:T(128)} %constant.20.clone.1), window={size=1x1x1x1x128 pad=0_0x0_0x0_0x0_0x127_0}, to_apply=%region_2.3 | reduce-window | flops 16646144 | bytes 1048580 | tf_op jit(solution)/shard_map/reduce-window
  104.6 0.2 slice.152
  104.8 1.1 copy.9
  105.9 0.8 fusion.32
  106.7 0.2 broadcast_add_fusion
  106.9 0.3 copy.11
  107.2 0.4 reduce_window_sum.35
  107.8 0.4 copy-done.9
  108.3 1.4 %select_select_fusion.1 = f32[4,8,16,128]{3,2,1,0:T(8,128)S(1)} fusion(f32[4,8,16,128]{3,2,1,0:T(8,128)} %collective-permute-done.14, f32[4,8,16,128]{3,2,1,0:T(8,128)} %collective-permute-done.13, f32[4,8,16,128]{3,2,1,0:T(8,128)S(1)} %collective-permute-done.12, f32[4,8,16,128]{3,2,1,0:T(8,128)S(1)} %get-tuple-element.20, ...), kind=kLoop, calls=%fused_computation.60 | loop fusion | flops 458752 | bytes 2098048 | tf_op jit(solution)/shard_map/jit(_where)/select_n | solution.py:81
  109.8 1.4 %select_select_fusion = f32[4,8,16,128]{3,2,1,0:T(8,128)S(1)} fusion(f32[4,8,16,128]{3,2,1,0:T(8,128)} %collective-permute-done.14, f32[4,8,16,128]{3,2,1,0:T(8,128)} %collective-permute-done.13, f32[4,8,16,128]{3,2,1,0:T(8,128)S(1)} %collective-permute-done.12, f32[4,8,16,128]{3,2,1,0:T(8,128)S(1)} %get-tuple-element.20, ...), kind=kLoop, calls=%fused_computation.59 | loop fusion | flops 458752 | bytes 2098048 | tf_op jit(solution)/shard_map/jit(_where)/select_n | solution.py:83
  111.2 0.2 pad_maximum_fusion
  111.4 0.5 slice.156
  111.9 0.2 copy-done.18
  112.1 0.4 pad_select_fusion.6
  112.5 0.5 slice.157
  112.9 0.2 copy-done.41
  113.1 0.6 pad_select_fusion.5
  113.8 0.5 slice.158
  114.2 0.2 copy-done.40
  114.4 0.4 pad_select_fusion.4
  114.9 0.5 slice.159
  115.3 0.2 copy-done.39
  115.5 0.4 pad_select_fusion.3
  116.0 0.5 slice.160
  116.4 0.2 copy-done.38
  116.6 0.4 pad_select_fusion.2
  117.0 0.5 slice.161
  117.6 0.4 pad_select_fusion.1
  118.1 0.5 slice.162
  118.5 0.2 copy-done.42
  118.7 0.4 pad_select_fusion
  119.1 0.5 copy-done.2
  119.7 1.2 fusion.8
  (116 shorter events, 1.6 us)
Async XLA Ops:
  0.6 24.2 %copy-start = (f32[4,8,16,128]{3,2,1,0:T(8,128)S(1)}, f32[4,8,16,128]{3,2,1,0:T(8,128)}, u32[]{:S(2)}) copy-start(f32[4,8,16,128]{3,2,1,0:T(8,128)} %param.4) | copy-start | bytes 786436
  0.6 24.2 %copy-start.1 = (f32[8,16,128]{2,1,0:T(8,128)S(1)}, f32[8,16,128]{2,1,0:T(8,128)}, u32[]{:S(2)}) copy-start(f32[8,16,128]{2,1,0:T(8,128)} %param.5) | copy-start | bytes 196612
  0.7 17.1 %copy-start.43 = (s32[8,16]{1,0:T(8,128)S(1)}, s32[8,16]{1,0:T(8,128)}, u32[]{:S(2)}) copy-start(s32[8,16]{1,0:T(8,128)} %param.6) | copy-start | bytes 1540
  0.7 57.1 %collective-permute-start.4 = (f32[4,8,16,128]{3,2,1,0:T(8,128)}, f32[4,8,16,128]{3,2,1,0:T(8,128)S(1)}, u32[]{:S(2)}, u32[]{:S(2)}) collective-permute-start(f32[4,8,16,128]{3,2,1,0:T(8,128)} %param.4), channel_id=1, source_target_pairs={{0,240},{16,0},{32,16},{48,32},{64,48},{80,64},{96,80},{112,96},{1... | collective-permute-start | bytes 786440 | tf_op jit(solution)/shard_map/ppermute | solution.py:26
  7.6 54.4 %collective-permute-start.7 = (f32[4,8,16,128]{3,2,1,0:T(8,128)}, f32[4,8,16,128]{3,2,1,0:T(8,128)S(1)}, u32[]{:S(2)}, u32[]{:S(2)}) collective-permute-start(f32[4,8,16,128]{3,2,1,0:T(8,128)} %param.4), channel_id=1, source_target_pairs={{0,16},{16,32},{32,48},{48,64},{64,80},{80,96},{96,112},{112,128},... | collective-permute-start | bytes 786440 | tf_op jit(solution)/shard_map/ppermute | solution.py:26
  8.9 15.9 %collective-permute-start.11 = (f32[5,8,16,1]{3,2,1,0:T(8,128)S(1)}, f32[5,8,16,1]{3,2,1,0:T(8,128)S(1)}, u32[]{:S(2)}, u32[]{:S(2)}) collective-permute-start(f32[5,8,16,1]{3,2,1,0:T(8,128)S(1)} %get-tuple-element.14), channel_id=1, source_target_pairs={{0,16},{16,32},{32,48},{48,64},{64,80},{80,96},{96,112},{112,128},... | collective-permute-start | bytes 7688 | tf_op jit(solution)/shard_map/ppermute | solution.py:16
  9.0 15.9 %collective-permute-start.10 = (f32[5,8,16,1]{3,2,1,0:T(8,128)S(1)}, f32[5,8,16,1]{3,2,1,0:T(8,128)S(1)}, u32[]{:S(2)}, u32[]{:S(2)}) collective-permute-start(f32[5,8,16,1]{3,2,1,0:T(8,128)S(1)} %get-tuple-element.13), channel_id=1, source_target_pairs={{16,0},{32,16},{48,32},{64,48},{80,64},{96,80},{112,96},{128,112},... | collective-permute-start | bytes 7688 | tf_op jit(solution)/shard_map/ppermute | solution.py:19
  14.2 43.4 %copy-start.3 = (f32[8,16,128]{2,1,0:T(8,128)S(1)}, f32[8,16,128]{2,1,0:T(8,128)}, u32[]{:S(2)}) copy-start(f32[8,16,128]{2,1,0:T(8,128)} %param.7) | copy-start | bytes 196612
  14.2 43.3 %collective-permute-start.18 = (f32[5,8,2,128]{3,2,1,0:T(2,128)S(1)}, f32[5,8,2,128]{3,2,1,0:T(2,128)S(1)}, u32[]{:S(2)}, u32[]{:S(2)}) collective-permute-start(f32[5,8,2,128]{3,2,1,0:T(2,128)S(1)} %get-tuple-element.18), channel_id=1, source_target_pairs={{0,1},{1,2},{2,3},{3,4},{4,5},{5,6},{6,7},{7,8},{8,9},{9,10},{10,1... | collective-permute-start | bytes 122888 | tf_op jit(solution)/shard_map/ppermute | solution.py:16
  18.4 67.5 %copy-start.8 = (pred[8,16]{1,0:T(8,128)(4,1)}, pred[8,16]{1,0:T(8,128)(4,1)S(1)}, u32[]{:S(2)}) copy-start(pred[8,16]{1,0:T(8,128)(4,1)S(1)} %get-tuple-element.40) | copy-start | bytes 388
  18.4 67.5 %copy-start.10 = (pred[8,16]{1,0:T(8,128)(4,1)}, pred[8,16]{1,0:T(8,128)(4,1)S(1)}, u32[]{:S(2)}) copy-start(pred[8,16]{1,0:T(8,128)(4,1)S(1)} %get-tuple-element.41) | copy-start | bytes 388
  18.4 67.4 %copy-start.12 = (pred[8,16]{1,0:T(8,128)(4,1)}, pred[8,16]{1,0:T(8,128)(4,1)S(1)}, u32[]{:S(2)}) copy-start(pred[8,16]{1,0:T(8,128)(4,1)S(1)} %get-tuple-element.42) | copy-start | bytes 388
  18.4 67.4 %copy-start.14 = (pred[8,16]{1,0:T(8,128)(4,1)}, pred[8,16]{1,0:T(8,128)(4,1)S(1)}, u32[]{:S(2)}) copy-start(pred[8,16]{1,0:T(8,128)(4,1)S(1)} %get-tuple-element.43) | copy-start | bytes 388
  18.4 67.4 %copy-start.16 = (pred[8,16]{1,0:T(8,128)(4,1)}, pred[8,16]{1,0:T(8,128)(4,1)S(1)}, u32[]{:S(2)}) copy-start(pred[8,16]{1,0:T(8,128)(4,1)S(1)} %get-tuple-element.44) | copy-start | bytes 388
  18.4 67.4 %copy-start.33 = (pred[8,16]{1,0:T(8,128)(4,1)}, pred[8,16]{1,0:T(8,128)(4,1)S(1)}, u32[]{:S(2)}) copy-start(pred[8,16]{1,0:T(8,128)(4,1)S(1)} %get-tuple-element.31) | copy-start | bytes 388
  18.4 67.4 %copy-start.35 = (pred[8,16]{1,0:T(8,128)(4,1)}, pred[8,16]{1,0:T(8,128)(4,1)S(1)}, u32[]{:S(2)}) copy-start(pred[8,16]{1,0:T(8,128)(4,1)S(1)} %get-tuple-element.38) | copy-start | bytes 388
  18.4 67.6 %copy-start.19 = (pred[8,16]{1,0:T(8,128)(4,1)}, pred[8,16]{1,0:T(8,128)(4,1)S(1)}, u32[]{:S(2)}) copy-start(pred[8,16]{1,0:T(8,128)(4,1)S(1)} %get-tuple-element.32) | copy-start | bytes 388
  18.5 67.6 %copy-start.21 = (pred[8,16]{1,0:T(8,128)(4,1)}, pred[8,16]{1,0:T(8,128)(4,1)S(1)}, u32[]{:S(2)}) copy-start(pred[8,16]{1,0:T(8,128)(4,1)S(1)} %get-tuple-element.33) | copy-start | bytes 388
  18.5 67.6 %copy-start.23 = (pred[8,16]{1,0:T(8,128)(4,1)}, pred[8,16]{1,0:T(8,128)(4,1)S(1)}, u32[]{:S(2)}) copy-start(pred[8,16]{1,0:T(8,128)(4,1)S(1)} %get-tuple-element.34) | copy-start | bytes 388
  18.5 67.6 %copy-start.25 = (pred[8,16]{1,0:T(8,128)(4,1)}, pred[8,16]{1,0:T(8,128)(4,1)S(1)}, u32[]{:S(2)}) copy-start(pred[8,16]{1,0:T(8,128)(4,1)S(1)} %get-tuple-element.35) | copy-start | bytes 388
  18.5 67.6 %copy-start.27 = (pred[8,16]{1,0:T(8,128)(4,1)}, pred[8,16]{1,0:T(8,128)(4,1)S(1)}, u32[]{:S(2)}) copy-start(pred[8,16]{1,0:T(8,128)(4,1)S(1)} %get-tuple-element.36) | copy-start | bytes 388
  18.5 67.6 %copy-start.29 = (pred[8,16]{1,0:T(8,128)(4,1)}, pred[8,16]{1,0:T(8,128)(4,1)S(1)}, u32[]{:S(2)}) copy-start(pred[8,16]{1,0:T(8,128)(4,1)S(1)} %get-tuple-element.37) | copy-start | bytes 388
  18.5 67.6 %copy-start.31 = (pred[8,16]{1,0:T(8,128)(4,1)}, pred[8,16]{1,0:T(8,128)(4,1)S(1)}, u32[]{:S(2)}) copy-start(pred[8,16]{1,0:T(8,128)(4,1)S(1)} %get-tuple-element.39) | copy-start | bytes 388
  25.2 5.9 %collective-permute-start.1 = (f32[4,8,16]{2,1,0:T(8,128)S(1)}, f32[4,8,16]{2,1,0:T(8,128)S(1)}, u32[]{:S(2)}, u32[]{:S(2)}) collective-permute-start(f32[4,8,16]{2,1,0:T(8,128)S(1)} %get-tuple-element.19), channel_id=1, source_target_pairs={{0,16},{16,32},{32,48},{48,64},{64,80},{80,96},{96,112},{112,128},... | collective-permute-start | bytes 6152 | tf_op jit(solution)/shard_map/ppermute | solution.py:26
  31.1 18.5 %collective-permute-start.2 = (f32[4,8,16]{2,1,0:T(8,128)S(1)}, f32[4,8,16]{2,1,0:T(8,128)S(1)}, u32[]{:S(2)}, u32[]{:S(2)}) collective-permute-start(f32[4,8,16]{2,1,0:T(8,128)S(1)} %collective-permute-done.1), channel_id=1, source_target_pairs={{0,16},{16,32},{32,48},{48,64},{64,80},{80,96},{96,112},{112,128},... | collective-permute-start | bytes 6152 | tf_op jit(solution)/shard_map/ppermute | solution.py:26
  45.5 5.6 %collective-permute-start = (f32[4,8,16]{2,1,0:T(8,128)S(1)}, f32[4,8,16]{2,1,0:T(8,128)S(1)}, u32[]{:S(2)}, u32[]{:S(2)}) collective-permute-start(f32[4,8,16]{2,1,0:T(8,128)S(1)} %get-tuple-element.19), channel_id=1, source_target_pairs={{0,240},{16,0},{32,16},{48,32},{64,48},{80,64},{96,80},{112,96},{1... | collective-permute-start | bytes 6152 | tf_op jit(solution)/shard_map/ppermute | solution.py:26
  49.7 5.8 %collective-permute-start.3 = (f32[4,8,16]{2,1,0:T(8,128)S(1)}, f32[4,8,16]{2,1,0:T(8,128)S(1)}, u32[]{:S(2)}, u32[]{:S(2)}) collective-permute-start(f32[4,8,16]{2,1,0:T(8,128)S(1)} %collective-permute-done.2), channel_id=1, source_target_pairs={{0,16},{16,32},{32,48},{48,64},{64,80},{80,96},{96,112},{112,128},... | collective-permute-start | bytes 6152 | tf_op jit(solution)/shard_map/ppermute | solution.py:26
  51.1 6.5 %collective-permute-start.19 = (f32[5,8,2,128]{3,2,1,0:T(2,128)S(1)}, f32[5,8,2,128]{3,2,1,0:T(2,128)S(1)}, u32[]{:S(2)}, u32[]{:S(2)}) collective-permute-start(f32[5,8,2,128]{3,2,1,0:T(2,128)S(1)} %get-tuple-element.17), channel_id=1, source_target_pairs={{1,0},{2,1},{3,2},{4,3},{5,4},{6,5},{7,6},{8,7},{9,8},{10,9},{11,1... | collective-permute-start | bytes 122888 | tf_op jit(solution)/shard_map/ppermute | solution.py:19
  55.5 8.6 %collective-permute-start.12 = (f32[4,8,16,128]{3,2,1,0:T(8,128)S(1)}, f32[4,8,16,128]{3,2,1,0:T(8,128)S(1)}, u32[]{:S(2)}, u32[]{:S(2)}) collective-permute-start(f32[4,8,16,128]{3,2,1,0:T(8,128)S(1)} %get-tuple-element.20), channel_id=1, source_target_pairs={{0,240},{16,0},{32,16},{48,32},{64,48},{80,64},{96,80},{112,96},{1... | collective-permute-start | bytes 786440 | tf_op jit(solution)/shard_map/ppermute | solution.py:26
  57.5 11.3 %collective-permute-start.15 = (f32[4,8,16,128]{3,2,1,0:T(8,128)S(1)}, f32[4,8,16,128]{3,2,1,0:T(8,128)S(1)}, u32[]{:S(2)}, u32[]{:S(2)}) collective-permute-start(f32[4,8,16,128]{3,2,1,0:T(8,128)S(1)} %get-tuple-element.20), channel_id=1, source_target_pairs={{0,16},{16,32},{32,48},{48,64},{64,80},{80,96},{96,112},{112,128},... | collective-permute-start | bytes 786440 | tf_op jit(solution)/shard_map/ppermute | solution.py:26
  57.8 11.9 %collective-permute-start.5 = (f32[4,8,16,128]{3,2,1,0:T(8,128)S(1)}, f32[4,8,16,128]{3,2,1,0:T(8,128)S(1)}, u32[]{:S(2)}, u32[]{:S(2)}) collective-permute-start(f32[4,8,16,128]{3,2,1,0:T(8,128)S(1)} %collective-permute-done.4), channel_id=1, source_target_pairs={{0,240},{16,0},{32,16},{48,32},{64,48},{80,64},{96,80},{112,96},{1... | collective-permute-start | bytes 786440 | tf_op jit(solution)/shard_map/ppermute | solution.py:26
  62.0 12.5 %collective-permute-start.8 = (f32[4,8,16,128]{3,2,1,0:T(8,128)S(1)}, f32[4,8,16,128]{3,2,1,0:T(8,128)S(1)}, u32[]{:S(2)}, u32[]{:S(2)}) collective-permute-start(f32[4,8,16,128]{3,2,1,0:T(8,128)S(1)} %collective-permute-done.7), channel_id=1, source_target_pairs={{0,16},{16,32},{32,48},{48,64},{64,80},{80,96},{96,112},{112,128},... | collective-permute-start | bytes 786440 | tf_op jit(solution)/shard_map/ppermute | solution.py:26
  64.1 11.4 %collective-permute-start.13 = (f32[4,8,16,128]{3,2,1,0:T(8,128)S(1)}, f32[4,8,16,128]{3,2,1,0:T(8,128)}, u32[]{:S(2)}, u32[]{:S(2)}) collective-permute-start(f32[4,8,16,128]{3,2,1,0:T(8,128)S(1)} %collective-permute-done.12), channel_id=1, source_target_pairs={{0,240},{16,0},{32,16},{48,32},{64,48},{80,64},{96,80},{112,96},{1... | collective-permute-start | bytes 786440 | tf_op jit(solution)/shard_map/ppermute | solution.py:26
  68.9 11.5 %collective-permute-start.16 = (f32[4,8,16,128]{3,2,1,0:T(8,128)S(1)}, f32[4,8,16,128]{3,2,1,0:T(8,128)}, u32[]{:S(2)}, u32[]{:S(2)}) collective-permute-start(f32[4,8,16,128]{3,2,1,0:T(8,128)S(1)} %collective-permute-done.15), channel_id=1, source_target_pairs={{0,16},{16,32},{32,48},{48,64},{64,80},{80,96},{96,112},{112,128},... | collective-permute-start | bytes 786440 | tf_op jit(solution)/shard_map/ppermute | solution.py:26
  69.7 11.4 %collective-permute-start.6 = (f32[4,8,16,128]{3,2,1,0:T(8,128)S(1)}, f32[4,8,16,128]{3,2,1,0:T(8,128)S(1)}, u32[]{:S(2)}, u32[]{:S(2)}) collective-permute-start(f32[4,8,16,128]{3,2,1,0:T(8,128)S(1)} %collective-permute-done.5), channel_id=1, source_target_pairs={{0,240},{16,0},{32,16},{48,32},{64,48},{80,64},{96,80},{112,96},{1... | collective-permute-start | bytes 786440 | tf_op jit(solution)/shard_map/ppermute | solution.py:26
  74.5 11.4 %collective-permute-start.9 = (f32[4,8,16,128]{3,2,1,0:T(8,128)S(1)}, f32[4,8,16,128]{3,2,1,0:T(8,128)S(1)}, u32[]{:S(2)}, u32[]{:S(2)}) collective-permute-start(f32[4,8,16,128]{3,2,1,0:T(8,128)S(1)} %collective-permute-done.8), channel_id=1, source_target_pairs={{0,16},{16,32},{32,48},{48,64},{64,80},{80,96},{96,112},{112,128},... | collective-permute-start | bytes 786440 | tf_op jit(solution)/shard_map/ppermute | solution.py:26
  75.5 32.3 %collective-permute-start.14 = (f32[4,8,16,128]{3,2,1,0:T(8,128)}, f32[4,8,16,128]{3,2,1,0:T(8,128)}, u32[]{:S(2)}, u32[]{:S(2)}) collective-permute-start(f32[4,8,16,128]{3,2,1,0:T(8,128)} %collective-permute-done.13), channel_id=1, source_target_pairs={{0,240},{16,0},{32,16},{48,32},{64,48},{80,64},{96,80},{112,96},{1... | collective-permute-start | bytes 786440 | tf_op jit(solution)/shard_map/ppermute | solution.py:26
  80.3 27.5 %collective-permute-start.17 = (f32[4,8,16,128]{3,2,1,0:T(8,128)}, f32[4,8,16,128]{3,2,1,0:T(8,128)}, u32[]{:S(2)}, u32[]{:S(2)}) collective-permute-start(f32[4,8,16,128]{3,2,1,0:T(8,128)} %collective-permute-done.16), channel_id=1, source_target_pairs={{0,16},{16,32},{32,48},{48,64},{64,80},{80,96},{96,112},{112,128},... | collective-permute-start | bytes 786440 | tf_op jit(solution)/shard_map/ppermute | solution.py:26
  107.6 0.7 copy-start.9
  107.6 0.7 copy-start.11
  107.6 0.7 copy-start.13
  107.6 0.7 copy-start.15
  107.6 0.7 copy-start.17
  107.7 0.7 copy-start.34
  107.7 0.7 copy-start.36
  107.7 2.0 %copy-start.20 = (pred[8,16]{1,0:T(8,128)(4,1)S(1)}, pred[8,16]{1,0:T(8,128)(4,1)}, u32[]{:S(2)}) copy-start(pred[8,16]{1,0:T(8,128)(4,1)} %copy-done.19) | copy-start | bytes 388
  107.7 2.0 %copy-start.22 = (pred[8,16]{1,0:T(8,128)(4,1)S(1)}, pred[8,16]{1,0:T(8,128)(4,1)}, u32[]{:S(2)}) copy-start(pred[8,16]{1,0:T(8,128)(4,1)} %copy-done.21) | copy-start | bytes 388
  107.7 2.0 %copy-start.24 = (pred[8,16]{1,0:T(8,128)(4,1)S(1)}, pred[8,16]{1,0:T(8,128)(4,1)}, u32[]{:S(2)}) copy-start(pred[8,16]{1,0:T(8,128)(4,1)} %copy-done.23) | copy-start | bytes 388
  107.7 2.0 %copy-start.26 = (pred[8,16]{1,0:T(8,128)(4,1)S(1)}, pred[8,16]{1,0:T(8,128)(4,1)}, u32[]{:S(2)}) copy-start(pred[8,16]{1,0:T(8,128)(4,1)} %copy-done.25) | copy-start | bytes 388
  107.7 2.0 %copy-start.28 = (pred[8,16]{1,0:T(8,128)(4,1)S(1)}, pred[8,16]{1,0:T(8,128)(4,1)}, u32[]{:S(2)}) copy-start(pred[8,16]{1,0:T(8,128)(4,1)} %copy-done.27) | copy-start | bytes 388
  107.7 2.0 %copy-start.30 = (pred[8,16]{1,0:T(8,128)(4,1)S(1)}, pred[8,16]{1,0:T(8,128)(4,1)}, u32[]{:S(2)}) copy-start(pred[8,16]{1,0:T(8,128)(4,1)} %copy-done.29) | copy-start | bytes 388
  107.7 2.0 %copy-start.32 = (pred[8,16]{1,0:T(8,128)(4,1)S(1)}, pred[8,16]{1,0:T(8,128)(4,1)}, u32[]{:S(2)}) copy-start(pred[8,16]{1,0:T(8,128)(4,1)} %copy-done.31) | copy-start | bytes 388
  111.4 0.7 copy-start.18
  112.5 0.7 copy-start.41
  113.8 0.7 copy-start.40
  114.9 0.7 copy-start.39
  115.9 0.7 copy-start.38
  117.0 0.6 copy-start.37
  118.1 0.6 copy-start.42
  118.7 0.9 copy-start.2
  118.7 1.0 copy-start.4
  118.7 1.0 copy-start.5
  118.7 1.0 copy-start.6
  118.7 1.0 copy-start.7
where the time goes:
time: 121 us
  other arithmetic  47.9 us (40%)
  starting transfers between devices  39.6 us (33%)
  waiting for transfers between devices  24.3 us (20%)
  local copies, waits for them, and re-layouts  7.72 us (6%)
  between operations  1.42 us (1%)
    ppermute x16, starting transfers between devices, passed_along(): lax.ppermute(array, axis, [(i, (i + by) % size) for i in range(size)])  31.3 us
    another operation x3, other arithmetic  19.1 us
    ppermute x16, waiting for transfers between devices, passed_along(): lax.ppermute(array, axis, [(i, (i + by) % size) for i in range(size)])  18.6 us
    another operation x1, other arithmetic, per_device(): own_incl = jnp.cumsum(tracers, axis=3)  14.4 us
    ppermute x2, starting transfers between devices, extended(): lax.ppermute(lax.slice_in_dim(block, 0, width, axis=dim), axis, backward)  6.12 us
    ppermute x2, waiting for transfers between devices, extended(): lax.ppermute(lax.slice_in_dim(block, block.shape[dim] - width, None, axis...  5.69 us
    slice x7, local copies, waits for them, and re-layouts, align_window(): current[..., step:]  3.29 us
    select_n x7, other arithmetic, align_window(): current = jnp.where(flag, moved, current)  3.1 us
  transfers between devices with their start and end apart: 20, of which 12 were waited for; matrix products, arithmetic and copies ran while one was open for 35% of the time, Pallas kernels for 0%

commit v1 on v0

v1 whole, which is shorter than its diff:
```python
import functools

import jax
import jax.numpy as jnp
from jax import lax
from jax.experimental import pallas as pl
from jax.experimental.pallas import tpu as pltpu
from jax.sharding import PartitionSpec as P

TR, LEV, ROWS, LON, RING, BANDS = 4, 8, 16, 128, 16, 16
HALF = 8
REACH = 3
MESH = pl.DeviceIdType.MESH
ORDER = tuple(z + 8 * y for z in range(8) for y in range(2))


def lanes_iota(rows):
    return lax.broadcasted_iota(jnp.int32, (rows, LON), 1)


def rows_iota(rows):
    return lax.broadcasted_iota(jnp.int32, (rows, LON), 0)


def take(values, index):
    return jnp.take_along_axis(values, index, axis=1, mode="promise_in_bounds")


def kernel(
    q_hbm, c_hbm, s_ref, v_hbm, upd_ref, flux_ref,
    qx, mx, cv, gat, ret, back, pack, base, cw_out, cw_in,
    s1, r1, s2, r2, sl, sh, rh, se, re,
):
    me = lax.axis_index("lon")
    lat = lax.axis_index("lat")
    east, west = lax.rem(me + 1, RING), lax.rem(me + RING - 1, RING)
    north, south = lax.rem(lat + 1, BANDS), lax.rem(lat + BANDS - 1, BANDS)

    barrier = pltpu.get_barrier_semaphore()
    for d in range(1, RING):
        pl.semaphore_signal(barrier, inc=1, device_id={"lon": lax.rem(me + d, RING)}, device_id_type=MESH)
    for peer in (north, south):
        pl.semaphore_signal(barrier, inc=1, device_id={"lat": peer}, device_id_type=MESH)

    def of_home(h):
        return q_hbm.at[:, h // 2, pl.ds(pl.multiple_of((h % 2) * HALF, HALF), HALF), :]

    own = pltpu.make_async_copy(of_home(me), gat.at[me], sl.at[0])
    own_q = pltpu.make_async_copy(q_hbm, qx.at[:, :, pl.ds(8, ROWS), :], sl.at[1])
    own_v = pltpu.make_async_copy(v_hbm, mx.at[:, pl.ds(8, ROWS), :], sl.at[2])
    own_c = pltpu.make_async_copy(c_hbm, cv, sl.at[3])
    own_c.start()
    own.start()
    own_q.start()
    own_v.start()
    pl.semaphore_wait(barrier, RING + 1)

    def gather_copy(d):
        target = lax.rem(me + d, RING)
        return pltpu.make_async_remote_copy(
            of_home(target), gat.at[me], s1.at[d], r1.at[d], device_id={"lon": target}, device_id_type=MESH
        )

    for d in range(1, RING):
        gather_copy(d).start()

    halo = [
        (q_hbm.at[:, :, pl.ds(ROWS - 2, 2), :], qx.at[:, :, pl.ds(6, 2), :], north),
        (q_hbm.at[:, :, pl.ds(0, 2), :], qx.at[:, :, pl.ds(24, 2), :], south),
        (v_hbm.at[:, pl.ds(ROWS - 1, 1), :], mx.at[:, pl.ds(7, 1), :], north),
    ]
    halo = [
        pltpu.make_async_remote_copy(a, b, sh.at[i], rh.at[i], device_id={"lat": p}, device_id_type=MESH)
        for i, (a, b, p) in enumerate(halo)
    ]
    for copy in halo:
        copy.start()

    lane8, row8 = lanes_iota(HALF), rows_iota(HALF)
    own_c.wait()
    packed = jnp.zeros((HALF, LON), jnp.float32)
    for tile in range(2 * LEV):
        column = cv[tile // 2, HALF * (tile % 2) : HALF * (tile % 2) + HALF, LON - 1 : LON]
        packed = jnp.where(lane8 == HALF * tile + row8, column, packed)
    cw_out[...] = jnp.broadcast_to(jnp.sum(packed, axis=0, keepdims=True), (HALF, LON))
    edge = pltpu.make_async_remote_copy(
        cw_out, cw_in, se.at[0], re.at[0], device_id={"lon": east}, device_id_type=MESH
    )
    edge.start()

    lev = me // 2
    line = s_ref[pl.ds(lev, 1), :].astype(jnp.float32)
    pick = lax.broadcasted_iota(jnp.int32, (HALF, ROWS), 1) == (
        lax.broadcasted_iota(jnp.int32, (HALF, ROWS), 0) + HALF * (me % 2)
    )
    shift = jnp.sum(jnp.where(pick, jnp.broadcast_to(line, (HALF, ROWS)), 0.0), axis=1, keepdims=True)
    first = -1 - jnp.broadcast_to(shift, (HALF, LON)).astype(jnp.int32)
    raised = first + REACH * LON
    low = jnp.right_shift(raised, 7)
    remain = jnp.bitwise_and(raised, LON - 1)
    hop = jnp.where(lane8 >= remain, low, low + 1)
    bits = [jnp.bitwise_and(hop, 1 << n) != 0 for n in range(3)]
    turn = jnp.bitwise_and(lane8 + remain, LON - 1)
    signs = []
    for off in range(-REACH, REACH):
        cell = off * LON + lane8
        if off < 0:
            signs.append(jnp.where(cell >= first, -1.0, 0.0))
        else:
            signs.append(jnp.where(cell < first, 1.0, 0.0))
    group = lane8 // (TR * HALF)
    ends = jnp.where(group == 0, LON - 1, jnp.where(group == 1, 0, 1))

    own.wait()
    for d in range(1, RING):
        gather_copy(d).wait_recv()

    def home(tr, carry):
        blocks = [gat[b, tr] for b in range(RING)]
        mine = (lane8 // HALF) % TR == tr
        mine = mine & (lane8 % HALF == row8)
        one = [jnp.where(bits[0], blocks[(b - 2) % RING], blocks[(b - 3) % RING]) for b in range(RING)]
        two = [jnp.where(bits[1], one[(b + 2) % RING], one[b]) for b in range(RING)]
        aligned = [take(jnp.where(bits[2], two[(b + 4) % RING], two[b]), turn) for b in range(RING)]
        tips = [take(a, ends) for a in aligned]
        rows = pl.ds(pl.multiple_of(tr * HALF, HALF), HALF)
        for b in range(RING):
            ret[b, rows, :] = aligned[b]
            total = blocks[(b - REACH) % RING] * signs[0]
            for n in range(1, 2 * REACH):
                total = total + blocks[(b - REACH + n) % RING] * signs[n]
            offset = jnp.sum(total, axis=1, keepdims=True)
            extra = jnp.where(group == 0, tips[b - 1], jnp.where(group == 3, offset, tips[(b + 1) % RING]))
            pack[b] = jnp.where(mine, extra, pack[b])
        return carry

    for b in range(RING):
        pack[b] = jnp.zeros((HALF, LON), jnp.float32)
    lax.fori_loop(0, TR, home, 0)
    for b in range(RING):
        ret[b, TR * HALF : TR * HALF + 1, :] = jnp.sum(pack[b], axis=0, keepdims=True)

    size = TR * HALF + 1

    def return_copy(t):
        return pltpu.make_async_remote_copy(
            ret.at[t, pl.ds(0, size)], back.at[me, pl.ds(0, size)], s2.at[t], r2.at[me],
            device_id={"lon": t}, device_id_type=MESH,
        )

    for t in ORDER:
        @pl.when(t != me)
        def _():
            return_copy(t).start()

    own_back = pltpu.make_async_copy(ret.at[me, pl.ds(0, size)], back.at[me, pl.ds(0, size)], r2.at[me])
    own_back.start()

    own_q.wait()
    own_v.wait()
    for copy in halo:
        copy.wait_recv()
    face = lat * ROWS + rows_iota(ROWS)

    def meridional(l, carry):
        for o in (-1, 0):
            v = mx[l, 8 + o : 24 + o]
            v = jnp.where((face + o == NLAT - 1) | (face + o < 0), 0.0, v)
            up = v >= 0.0
            half_low = v * (1.0 - v) * 0.5
            half_high = v * (1.0 + v) * 0.5
            zero_low = (face + o <= 0) | (face + o >= NLAT - 1)
            zero_high = (face + o + 1 <= 0) | (face + o + 1 >= NLAT - 1)
            for tr in range(TR):
                q_low = qx[tr, l, 8 + o : 24 + o]
                q_high = qx[tr, l, 9 + o : 25 + o]
                side_low = jnp.where(zero_low, 0.0, 0.5 * (q_high - qx[tr, l, 7 + o : 23 + o]))
                side_high = jnp.where(zero_high, 0.0, 0.5 * (qx[tr, l, 10 + o : 26 + o] - q_low))
                flux = jnp.where(up, v * q_low + half_low * side_low, v * q_high - half_high * side_high)
                if o < 0:
                    base[tr, l] = qx[tr, l, 8:24] + flux
                else:
                    base[tr, l] = base[tr, l] - flux
        return carry

    lax.fori_loop(0, LEV, meridional, 0)

    edge.wait_recv()
    west_row = jnp.broadcast_to(cw_in[0:1, :], (HALF, LON))
    upper = jnp.where(
        lax.broadcasted_iota(jnp.int32, (LON, LON), 0) <= lax.broadcasted_iota(jnp.int32, (LON, LON), 1), 1.0, 0.0
    ).astype(jnp.bfloat16)
    lane32, row32 = lanes_iota(TR * HALF), rows_iota(TR * HALF)
    index_a = jnp.where(lane32 == LON - 2, 1, jnp.where(lane32 == LON - 1, 2, 0)) * (TR * HALF) + row32
    index_b = jnp.where(lane32 == LON - 1, 1, 3) * (TR * HALF) + row32

    def finish(h, carry):
        pltpu.make_async_copy(ret.at[h, pl.ds(0, size)], back.at[h, pl.ds(0, size)], r2.at[h]).wait()
        l = h // 2
        start = pl.multiple_of((h % 2) * HALF, HALF)
        cells = back[h, 0 : TR * HALF]
        extra = jnp.broadcast_to(back[h, TR * HALF : TR * HALF + 1], (TR * HALF, LON))
        ext_a, ext_b = take(extra, index_a), take(extra, index_b)
        plus1 = jnp.where(lane32 == LON - 1, ext_b, pltpu.roll(cells, LON - 1, 1))
        plus2 = jnp.where(lane32 >= LON - 2, ext_a, pltpu.roll(cells, LON - 2, 1))
        q = jnp.concatenate([qx[tr, l, pl.ds(start + 8, HALF), :] for tr in range(TR)], axis=0)
        diff = q - cells
        part0 = diff.astype(jnp.bfloat16)
        rest = diff - part0.astype(jnp.float32)
        part1 = rest.astype(jnp.bfloat16)
        part2 = (rest - part1.astype(jnp.float32)).astype(jnp.bfloat16)
        sums = (
            jnp.dot(part2, upper, preferred_element_type=jnp.float32)
            + jnp.dot(part1, upper, preferred_element_type=jnp.float32)
        ) + jnp.dot(part0, upper, preferred_element_type=jnp.float32)
        c = cv[l, pl.ds(start, HALF), :]
        t = 1.0 - c
        tt = (t * t - t) * 0.25
        t_west = 1.0 - take(west_row, HALF * h + row8)
        tt_west = (t_west * t_west - t_west) * 0.25
        t, tt, t_west, tt_west = (jnp.concatenate([x] * TR, axis=0) for x in (t, tt, t_west, tt_west))
        offset = jnp.broadcast_to(ext_b[:, 0:1], (TR * HALF, LON))
        flux = sums - offset - (plus1 * t + (plus2 - cells) * tt)
        first_west = -ext_b - (cells * t_west + (plus1 - ext_a) * tt_west)
        flux_west = jnp.where(lane32 == 0, first_west, pltpu.roll(flux, 1, 1))
        change = flux - flux_west
        for tr in range(TR):
            rows = slice(tr * HALF, (tr + 1) * HALF)
            flux_ref[tr, l, pl.ds(start, HALF), :] = flux[rows]
            upd_ref[tr, l, pl.ds(start, HALF), :] = base[tr, l, pl.ds(start, HALF), :] - change[rows]
        return carry

    lax.fori_loop(0, RING, finish, 0)

    for d in range(1, RING):
        gather_copy(d).wait_send()
    for copy in halo:
        copy.wait_send()
    edge.wait_send()
    for t in ORDER:
        @pl.when(t != me)
        def _():
            return_copy(t).wait_send()


NLAT = ROWS * BANDS


def per_device(tracers, courant_frac, shifts, merid):
    vmem, dma, f32 = pltpu.VMEM, pltpu.SemaphoreType.DMA, jnp.float32
    shape = jax.ShapeDtypeStruct((TR, LEV, ROWS, LON), f32)
    anywhere, inside = pl.BlockSpec(memory_space=pl.ANY), pl.BlockSpec(memory_space=pltpu.VMEM)
    return pl.pallas_call(
        kernel,
        out_shape=(shape, shape),
        in_specs=[anywhere, anywhere, inside, anywhere],
        out_specs=(inside, inside),
        scratch_shapes=[
            vmem((TR, LEV, 32, LON), f32),
            vmem((LEV, 32, LON), f32),
            vmem((LEV, ROWS, LON), f32),
            vmem((RING, TR, HALF, LON), f32),
            vmem((RING, 40, LON), f32),
            vmem((RING, 40, LON), f32),
            vmem((RING, HALF, LON), f32),
            vmem((TR, LEV, ROWS, LON), f32),
            vmem((HALF, LON), f32),
            vmem((HALF, LON), f32),
            dma((RING,)), dma((RING,)), dma((RING,)), dma((RING,)), dma((4,)), dma((3,)), dma((3,)), dma((1,)), dma((1,)),
        ],
        compiler_params=pltpu.CompilerParams(collective_id=0, has_side_effects=True),
        cost_estimate=pl.CostEstimate(flops=100_000_000, bytes_accessed=1_000_000, transcendentals=0),
    )(tracers, courant_frac, shifts, merid)


def solution(mesh):
    return jax.shard_map(
        per_device,
        mesh=mesh,
        in_specs=(
            P(None, None, "lat", "lon"),
            P(None, "lat", "lon"),
            P(None, "lat"),
            P(None, "lat", "lon"),
        ),
        out_specs=(P(None, None, "lat", "lon"), P(None, None, "lat", "lon")),
        check_vma=False,
    )
```

time: 121 us -> 32.1 us (0.27)
  other arithmetic: 47.9 us -> 0 us
  starting transfers between devices: 39.6 us -> 0 us
  Pallas kernels: 0 us -> 28.4 us
  waiting for transfers between devices: 24.3 us -> 0 us
  local copies, waits for them, and re-layouts: 7.72 us -> 2.42 us
    ppermute x20 -> x0, starting transfers between devices: 39.6 us -> none  [the longest x16 31.3 us: passed_along(): lax.ppermute(array, axis, [(i, (i + by) % size) for i in range(size)])]
    another operation x6 -> x0, other arithmetic: 33.7 us -> none
    pallas_call x0 -> x1, Pallas kernels: none -> 28.4 us  [per_device(): pl.pallas_call(kernel, out_shape=(shape, shape), in_specs=[anywhere, anyw...]
    ppermute x20 -> x0, waiting for transfers between devices: 24.3 us -> none  [the longest x16 18.6 us: passed_along(): lax.ppermute(array, axis, [(i, (i + by) % size) for i in range(size)])]
    select_n x14 -> x0, other arithmetic: 6.59 us -> none  [the longest x7 3.1 us: align_window(): current = jnp.where(flag, moved, current)]
    slice x9 -> x0, local copies, waits for them, and re-layouts: 4.55 us -> none  [the longest x7 3.29 us: align_window(): current[..., step:]]
    sub x3 -> x0, other arithmetic: 2.75 us -> none  [the longest x1 1.52 us: per_device(): weight_east = 1.0 - courant_frac]
    concatenate x3 -> x0, other arithmetic: 2.37 us -> none  [the longest x1 1.26 us: per_device(): stacked = jnp.concatenate((tracers, courant_frac[None]), axis=0)]
  transfers between devices with their start and end apart: 20 -> 0, of which waited for: 12 -> 0; matrix products, arithmetic and copies ran while one was open for 35% -> 0% of each run, Pallas kernels for 0% -> 0%
where the time goes in v1:
time: 32.1 us; the launch traced here: 31.5 us
  Pallas kernels  28.4 us (88%)
  local copies, waits for them, and re-layouts  2.42 us (8%)
  between operations  0.65 us (2%)
    pallas_call x1, Pallas kernels, per_device(): pl.pallas_call(kernel, out_shape=(shape, shape), in_specs=[anywhere, anyw...  28.4 us
    unnamed x4, local copies, waits for them, and re-layouts  2.42 us

profile of v1, /device:TPU:6, one launch (start us, length us, event | category | flops | bytes accessed | tf_op | source)
XLA Modules:
  0.0 31.5 jit_solution(13844482657397414858)
XLA Ops:
  0.6 28.4 %shard_map.59 = (f32[4,8,16,128]{3,2,1,0:T(8,128)}, f32[4,8,16,128]{3,2,1,0:T(8,128)}) custom-call(f32[4,8,16,128]{3,2,1,0:T(8,128)} %q_hbm.1, f32[8,16,128]{2,1,0:T(8,128)} %c_hbm.1, s32[8,16]{1,0:T(8,128)} %s_ref.1, f32[8,16,128]{2,1,0:T(8,128)} %v_hbm.1), custom_call_target="tpu_custom_call" | custom-call | flops 100000000 | bytes 1000000 | tf_op jit(solution)/shard_map/pallas_call | solution.py:253
  29.1 0.0 copy-start
  29.1 1.7 %copy.8 = f32[4,8,16,128]{3,2,1,0:T(8,128)} copy(f32[4,8,16,128]{3,2,1,0:T(8,128)} %get-tuple-element.4) | data formatting | bytes 524288
  30.8 0.0 copy-done
  30.8 0.7 %copy.9 = f32[4,8,16,128]{3,2,1,0:T(8,128)} copy(f32[4,8,16,128]{3,2,1,0:T(8,128)S(1)} %copy-done) | data formatting | bytes 524288
Async XLA Ops:
  29.1 1.7 %copy-start = (f32[4,8,16,128]{3,2,1,0:T(8,128)S(1)}, f32[4,8,16,128]{3,2,1,0:T(8,128)}, u32[]{:S(2)}) copy-start(f32[4,8,16,128]{3,2,1,0:T(8,128)} %get-tuple-element.5) | copy-start | bytes 786436

commit v2 on v1

v2 whole, which is shorter than its diff:
```python
import functools

import jax
import jax.numpy as jnp
from jax import lax
from jax.experimental import pallas as pl
from jax.experimental.pallas import tpu as pltpu
from jax.sharding import PartitionSpec as P

TR, LEV, ROWS, LON, RING, BANDS = 4, 8, 16, 128, 16, 16
NLAT = ROWS * BANDS
HALF = 8
REACH = 3
PARTS = 2
EACH = TR // PARTS
WIDE = EACH * HALF
SIZE = WIDE + 1
MESH = pl.DeviceIdType.MESH
FAR = tuple(sorted(range(1, RING), key=lambda d: (-min(d % 8, 8 - d % 8), d)))
ORDER = tuple(z + 8 * y for z in range(8) for y in range(2))


def lanes_iota(rows):
    return lax.broadcasted_iota(jnp.int32, (rows, LON), 1)


def rows_iota(rows):
    return lax.broadcasted_iota(jnp.int32, (rows, LON), 0)


def take(values, index):
    return jnp.take_along_axis(values, index, axis=1, mode="promise_in_bounds")


def ring(index):
    return jnp.bitwise_and(index, RING - 1)


def kernel(
    q_hbm, c_hbm, s_hbm, v_hbm, upd_hbm, flux_hbm,
    s_ref, qx, mx, cv, gat, ret, back, pack, base, flux_v, cw_out, cw_in,
    s1, r1, s2, r2, sl, sh, rh, se, re, so,
):
    me = lax.axis_index("lon")
    lat = lax.axis_index("lat")

    barrier = pltpu.get_barrier_semaphore()
    for d in FAR:
        pl.semaphore_signal(barrier, inc=1, device_id={"lon": ring(me + d)}, device_id_type=MESH)
    north, south = ring(lat + 1), ring(lat + BANDS - 1)
    for peer in (north, south):
        pl.semaphore_signal(barrier, inc=1, device_id={"lat": peer}, device_id_type=MESH)

    def of_home(h, part):
        rows = pl.ds(pl.multiple_of(HALF + (h % 2) * HALF, HALF), HALF)
        return qx.at[pl.ds(part * EACH, EACH), h // 2, rows, :]

    own_q = pltpu.make_async_copy(q_hbm, qx.at[:, :, pl.ds(8, ROWS), :], sl.at[0])
    own_s = pltpu.make_async_copy(s_hbm, s_ref, sl.at[1])
    own_c = pltpu.make_async_copy(c_hbm, cv, sl.at[2])
    own_v = pltpu.make_async_copy(v_hbm, mx.at[:, pl.ds(8, ROWS), :], sl.at[3])
    for copy in (own_q, own_s, own_c, own_v):
        copy.start()
    own_q.wait()
    own = [pltpu.make_async_copy(of_home(me, p), gat.at[me, pl.ds(p * EACH, EACH)], sl.at[4 + p]) for p in range(PARTS)]
    for copy in own:
        copy.start()

    lane8, row8 = lanes_iota(HALF), rows_iota(HALF)
    own_s.wait()
    line = s_ref[pl.ds(me // 2, 1), :].astype(jnp.float32)
    pick = lax.broadcasted_iota(jnp.int32, (HALF, ROWS), 1) == (
        lax.broadcasted_iota(jnp.int32, (HALF, ROWS), 0) + HALF * (me % 2)
    )
    shift = jnp.sum(jnp.where(pick, jnp.broadcast_to(line, (HALF, ROWS)), 0.0), axis=1, keepdims=True)
    first = -1 - jnp.broadcast_to(shift, (HALF, LON)).astype(jnp.int32)
    raised = first + REACH * LON
    low = jnp.right_shift(raised, 7)
    remain = jnp.bitwise_and(raised, LON - 1)
    hop = jnp.where(lane8 >= remain, low, low + 1)
    bits = [jnp.bitwise_and(hop, 1 << n) != 0 for n in range(3)]
    turn = jnp.bitwise_and(lane8 + remain, LON - 1)
    signs = []
    for off in range(-REACH, REACH):
        cell = off * LON + lane8
        if off < 0:
            signs.append(jnp.where(cell >= first, -1.0, 0.0))
        else:
            signs.append(jnp.where(cell < first, 1.0, 0.0))
    group = lane8 // WIDE
    ends = jnp.where(group == 0, LON - 1, jnp.where(group == 1, 0, 1))

    own_c.wait()
    packed = jnp.zeros((HALF, LON), jnp.float32)
    for tile in range(2 * LEV):
        column = cv[tile // 2, HALF * (tile % 2) : HALF * (tile % 2) + HALF, LON - 1 : LON]
        packed = jnp.where(lane8 == HALF * tile + row8, column, packed)
    cw_out[...] = jnp.broadcast_to(jnp.sum(packed, axis=0, keepdims=True), (HALF, LON))

    pl.semaphore_wait(barrier, RING + 1)

    def gather_copy(d, part):
        target = ring(me + d)
        return pltpu.make_async_remote_copy(
            of_home(target, part), gat.at[me, pl.ds(part * EACH, EACH)], s1.at[part, d], r1.at[part, d],
            device_id={"lon": target}, device_id_type=MESH,
        )

    for part in range(PARTS):
        for d in FAR:
            gather_copy(d, part).start()

    halo = [
        (q_hbm.at[:, :, pl.ds(ROWS - 2, 2), :], qx.at[:, :, pl.ds(6, 2), :], north),
        (q_hbm.at[:, :, pl.ds(0, 2), :], qx.at[:, :, pl.ds(24, 2), :], south),
        (v_hbm.at[:, pl.ds(ROWS - 1, 1), :], mx.at[:, pl.ds(7, 1), :], north),
    ]
    halo = [
        pltpu.make_async_remote_copy(a, b, sh.at[i], rh.at[i], device_id={"lat": p}, device_id_type=MESH)
        for i, (a, b, p) in enumerate(halo)
    ]
    for copy in halo:
        copy.start()
    edge = pltpu.make_async_remote_copy(
        cw_out, cw_in, se.at[0], re.at[0], device_id={"lon": ring(me + 1)}, device_id_type=MESH
    )
    edge.start()

    own_v.wait()
    for copy in halo:
        copy.wait_recv()
    face = lat * ROWS + rows_iota(ROWS)

    def meridional(l, carry):
        for o in (-1, 0):
            v = mx[l, 8 + o : 24 + o]
            v = jnp.where((face + o == NLAT - 1) | (face + o < 0), 0.0, v)
            up = v >= 0.0
            half_low = v * (1.0 - v) * 0.5
            half_high = v * (1.0 + v) * 0.5
            zero_low = (face + o <= 0) | (face + o >= NLAT - 1)
            zero_high = (face + o + 1 <= 0) | (face + o + 1 >= NLAT - 1)
            for tr in range(TR):
                q_low = qx[tr, l, 8 + o : 24 + o]
                q_high = qx[tr, l, 9 + o : 25 + o]
                side_low = jnp.where(zero_low, 0.0, 0.5 * (q_high - qx[tr, l, 7 + o : 23 + o]))
                side_high = jnp.where(zero_high, 0.0, 0.5 * (qx[tr, l, 10 + o : 26 + o] - q_low))
                flux = jnp.where(up, v * q_low + half_low * side_low, v * q_high - half_high * side_high)
                if o < 0:
                    base[tr, l] = qx[tr, l, 8:24] + flux
                else:
                    base[tr, l] = base[tr, l] - flux
        return carry

    lax.fori_loop(0, LEV, meridional, 0)

    def return_copy(t, part):
        return pltpu.make_async_remote_copy(
            ret.at[part, t, pl.ds(0, SIZE)], back.at[part, me, pl.ds(0, SIZE)], s2.at[part, t], r2.at[part, me],
            device_id={"lon": t}, device_id_type=MESH,
        )

    for part in range(PARTS):
        own[part].wait()
        for d in FAR[::-1]:
            gather_copy(d, part).wait_recv()

        rows_of = []
        for i in range(EACH):
            tr = part * EACH + i
            blocks = [gat[b, tr] for b in range(RING)]
            mine = ((lane8 // HALF) % EACH == i) & (lane8 % HALF == row8)
            one = [jnp.where(bits[0], blocks[(b - 2) % RING], blocks[(b - 3) % RING]) for b in range(RING)]
            two = [jnp.where(bits[1], one[(b + 2) % RING], one[b]) for b in range(RING)]
            aligned = [take(jnp.where(bits[2], two[(b + 4) % RING], two[b]), turn) for b in range(RING)]
            tips = [take(a, ends) for a in aligned]
            for b in range(RING):
                ret[part, b, HALF * i : HALF * i + HALF, :] = aligned[b]
                total = blocks[(b - REACH) % RING] * signs[0]
                for n in range(1, 2 * REACH):
                    total = total + blocks[(b - REACH + n) % RING] * signs[n]
                offset = jnp.sum(total, axis=1, keepdims=True)
                extra = jnp.where(group == 0, tips[b - 1], jnp.where(group == 3, offset, tips[(b + 1) % RING]))
                if i == 0:
                    pack[b] = jnp.where(mine, extra, 0.0)
                else:
                    pack[b] = jnp.where(mine, extra, pack[b])
        for b in range(RING):
            ret[part, b, WIDE:SIZE, :] = jnp.sum(pack[b], axis=0, keepdims=True)

        for t in ORDER:
            @pl.when(t != me)
            def _():
                return_copy(t, part).start()

        pltpu.make_async_copy(
            ret.at[part, me, pl.ds(0, SIZE)], back.at[part, me, pl.ds(0, SIZE)], r2.at[part, me]
        ).start()

    edge.wait_recv()
    west_row = jnp.broadcast_to(cw_in[0:1, :], (HALF, LON))
    upper = jnp.where(
        lax.broadcasted_iota(jnp.int32, (LON, LON), 0) <= lax.broadcasted_iota(jnp.int32, (LON, LON), 1), 1.0, 0.0
    ).astype(jnp.bfloat16)
    rows = 4 * WIDE
    lane, row = lanes_iota(rows), rows_iota(rows) % WIDE
    index_a = jnp.where(lane == LON - 2, 1, jnp.where(lane == LON - 1, 2, 0)) * WIDE + row
    index_b = jnp.where(lane == LON - 1, 1, 3) * WIDE + row

    def finish(part, d):
        past = jnp.where(d == 4, 4, 0)
        homes = [ring(me + d), ring(me + RING - d), ring(me + 8 + d + past), ring(me + 8 - d + past)]
        places = [(h // 2, pl.multiple_of((h % 2) * HALF, HALF)) for h in homes]
        for h in homes:
            pltpu.make_async_copy(
                ret.at[part, h, pl.ds(0, SIZE)], back.at[part, h, pl.ds(0, SIZE)], r2.at[part, h]
            ).wait()
        cells = jnp.concatenate([back[part, h, 0:WIDE] for h in homes], axis=0)
        extra = jnp.concatenate(
            [jnp.broadcast_to(back[part, h, WIDE:SIZE], (WIDE, LON)) for h in homes], axis=0
        )
        ext_a, ext_b = take(extra, index_a), take(extra, index_b)
        plus1 = jnp.where(lane == LON - 1, ext_b, pltpu.roll(cells, LON - 1, 1))
        plus2 = jnp.where(lane >= LON - 2, ext_a, pltpu.roll(cells, LON - 2, 1))
        q = jnp.concatenate(
            [qx[part * EACH + i, l, pl.ds(start + 8, HALF), :] for l, start in places for i in range(EACH)], axis=0
        )
        diff = q - cells
        part0 = diff.astype(jnp.bfloat16)
        rest = diff - part0.astype(jnp.float32)
        part1 = rest.astype(jnp.bfloat16)
        part2 = (rest - part1.astype(jnp.float32)).astype(jnp.bfloat16)
        sums = (
            jnp.dot(part2, upper, preferred_element_type=jnp.float32)
            + jnp.dot(part1, upper, preferred_element_type=jnp.float32)
        ) + jnp.dot(part0, upper, preferred_element_type=jnp.float32)
        frac = [cv[l, pl.ds(start, HALF), :] for l, start in places]
        west = [take(west_row, HALF * h + row8) for h in homes]
        weights = []
        for c in (frac, west):
            t = [1.0 - x for x in c]
            tt = [(x * x - x) * 0.25 for x in t]
            for w in (t, tt):
                weights.append(jnp.concatenate([x for x in w for _ in range(EACH)], axis=0))
        t, tt, t_west, tt_west = weights
        offset = jnp.broadcast_to(ext_b[:, 0:1], (rows, LON))
        flux = sums - offset - (plus1 * t + (plus2 - cells) * tt)
        first_west = -ext_b - (cells * t_west + (plus1 - ext_a) * tt_west)
        flux_west = jnp.where(lane == 0, first_west, pltpu.roll(flux, 1, 1))
        change = flux - flux_west
        at = 0
        for l, start in places:
            for i in range(EACH):
                spot = (part * EACH + i, l, pl.ds(start, HALF), slice(None))
                flux_v[spot] = flux[at : at + HALF]
                base[spot] = base[spot] - change[at : at + HALF]
                at += HALF

    written = []
    for part in range(PARTS):
        def step(d, carry):
            finish(part, d)
            return carry

        lax.fori_loop(1, 5, step, 0)
        some = pl.ds(part * EACH, EACH)
        for i, (src, dst) in enumerate(((flux_v, flux_hbm), (base, upd_hbm))):
            copy = pltpu.make_async_copy(src.at[some], dst.at[some], so.at[part, i])
            copy.start()
            written.append(copy)

    for part in range(PARTS):
        for d in FAR:
            gather_copy(d, part).wait_send()
        for t in ORDER:
            @pl.when(t != me)
            def _():
                return_copy(t, part).wait_send()
    for copy in halo:
        copy.wait_send()
    edge.wait_send()
    for copy in written:
        copy.wait()


def hand_on(upd_in, flux_in, upd_out, flux_out, upd_v, flux_v, arrived, gone):
    legs = []
    for i, (src, mid, dst) in enumerate(((upd_in, upd_v, upd_out), (flux_in, flux_v, flux_out))):
        for tr in range(TR):
            legs.append((
                pltpu.make_async_copy(src.at[tr], mid.at[tr], arrived.at[i, tr]),
                pltpu.make_async_copy(mid.at[tr], dst.at[tr], gone.at[i, tr]),
            ))
    for first, _ in legs:
        first.start()
    for first, second in legs:
        first.wait()
        second.start()
    for _, second in legs:
        second.wait()


def per_device(tracers, courant_frac, shifts, merid):
    vmem, dma, f32 = pltpu.VMEM, pltpu.SemaphoreType.DMA, jnp.float32
    shape = jax.ShapeDtypeStruct((TR, LEV, ROWS, LON), f32)
    anywhere = pl.BlockSpec(memory_space=pl.ANY)
    tall = -(-SIZE // 8) * 8
    updated, flux = pl.pallas_call(
        kernel,
        out_shape=(shape, shape),
        in_specs=[anywhere] * 4,
        out_specs=(anywhere, anywhere),
        scratch_shapes=[
            vmem((LEV, ROWS), jnp.int32),
            vmem((TR, LEV, 32, LON), f32),
            vmem((LEV, 32, LON), f32),
            vmem((LEV, ROWS, LON), f32),
            vmem((RING, TR, HALF, LON), f32),
            vmem((PARTS, RING, tall, LON), f32),
            vmem((PARTS, RING, tall, LON), f32),
            vmem((RING, HALF, LON), f32),
            vmem((TR, LEV, ROWS, LON), f32),
            vmem((TR, LEV, ROWS, LON), f32),
            vmem((HALF, LON), f32),
            vmem((HALF, LON), f32),
            dma((PARTS, RING)), dma((PARTS, RING)), dma((PARTS, RING)), dma((PARTS, RING)),
            dma((4 + PARTS,)), dma((3,)), dma((3,)), dma((1,)), dma((1,)), dma((PARTS, 2)),
        ],
        compiler_params=pltpu.CompilerParams(collective_id=0, has_side_effects=True),
        cost_estimate=pl.CostEstimate(flops=100_000_000, bytes_accessed=1_000_000, transcendentals=0),
    )(tracers, courant_frac, shifts, merid)
    whole = vmem((TR, LEV, ROWS, LON), f32)
    return pl.pallas_call(
        hand_on,
        out_shape=(shape, shape),
        in_specs=[anywhere] * 2,
        out_specs=(anywhere, anywhere),
        scratch_shapes=[whole, whole, dma((2, TR)), dma((2, TR))],
        cost_estimate=pl.CostEstimate(flops=0, bytes_accessed=2_000_000, transcendentals=0),
    )(updated, flux)


def solution(mesh):
    return jax.shard_map(
        per_device,
        mesh=mesh,
        in_specs=(
            P(None, None, "lat", "lon"),
            P(None, "lat", "lon"),
            P(None, "lat"),
            P(None, "lat", "lon"),
        ),
        out_specs=(P(None, None, "lat", "lon"), P(None, None, "lat", "lon")),
        check_vma=False,
    )
```

time: 32.1 us -> 28.2 us (0.88); the launches traced: 31.5 us -> 28 us
  local copies, waits for them, and re-layouts: 2.42 us -> 0 us
  Pallas kernels: 28.4 us -> 27.4 us
    unnamed x4 -> x0, local copies, waits for them, and re-layouts: 2.42 us -> none
    pallas_call x1 -> x2, Pallas kernels: 28.4 us -> 27.4 us  [the longest x1 25.6 us: per_device(): pl.pallas_call(kernel, out_shape=(shape, shape), in_specs=[anywhere] * 4,...]
where the time goes in v2:
time: 28.2 us; the launch traced here: 28 us
  Pallas kernels  27.4 us (97%)
  between operations  0.64 us (2%)
    pallas_call x1, Pallas kernels, per_device(): pl.pallas_call(kernel, out_shape=(shape, shape), in_specs=[anywhere] * 4,...  25.6 us
    pallas_call x1, Pallas kernels, per_device(): pl.pallas_call(hand_on, out_shape=(shape, shape), in_specs=[anywhere] * 2...  1.83 us

profile of v2, /device:TPU:6, one launch (start us, length us, event | category | flops | bytes accessed | tf_op | source)
XLA Modules:
  0.0 28.0 jit_solution(18381186449003405294)
XLA Ops:
  0.6 25.6 %shard_map.59 = (f32[4,8,16,128]{3,2,1,0:T(8,128)}, f32[4,8,16,128]{3,2,1,0:T(8,128)}) custom-call(f32[4,8,16,128]{3,2,1,0:T(8,128)} %q_hbm.1, f32[8,16,128]{2,1,0:T(8,128)} %c_hbm.1, s32[8,16]{1,0:T(8,128)} %s_hbm.1, f32[8,16,128]{2,1,0:T(8,128)} %v_hbm.1), custom_call_target="tpu_custom_call" | custom-call | flops 100000000 | bytes 1000000 | tf_op jit(solution)/shard_map/pallas_call | solution.py:308
  26.2 1.8 %shard_map.60 = (f32[4,8,16,128]{3,2,1,0:T(8,128)}, f32[4,8,16,128]{3,2,1,0:T(8,128)}) custom-call(f32[4,8,16,128]{3,2,1,0:T(8,128)} %get-tuple-element.4.upd_in, f32[4,8,16,128]{3,2,1,0:T(8,128)} %get-tuple-element.5.flux_in), custom_call_target="tpu_custom_call" | custom-call | bytes 2000000 | tf_op jit(solution)/shard_map/pallas_call | solution.py:333

commit v3 on v2

--- a/solution.py
+++ b/solution.py
@@ -16,8 +16,8 @@
 WIDE = EACH * HALF
 SIZE = WIDE + 1
 MESH = pl.DeviceIdType.MESH
-FAR = tuple(sorted(range(1, RING), key=lambda d: (-min(d % 8, 8 - d % 8), d)))
-ORDER = tuple(z + 8 * y for z in range(8) for y in range(2))
+FAR = tuple(sorted(range(RING), key=lambda d: (-min(d % 8, 8 - d % 8), d)))
+ORDER = (0, 8, 9, 1, 2, 10, 3, 11, 7, 15, 6, 14, 4, 12, 5, 13)
 
 
 def lanes_iota(rows):
@@ -37,37 +37,76 @@
 
 
 def kernel(
-    q_hbm, c_hbm, s_hbm, v_hbm, upd_hbm, flux_hbm,
-    s_ref, qx, mx, cv, gat, ret, back, pack, base, flux_v, cw_out, cw_in,
-    s1, r1, s2, r2, sl, sh, rh, se, re, so,
+    q_hbm, c_hbm, s_hbm, v_hbm, base, flux_v,
+    s_ref, qx, mx, cv, gat, ret, back, pack, cw_out, cw_in,
+    s1, r1, s2, r2, sl, sh, rh, se, re,
 ):
     me = lax.axis_index("lon")
     lat = lax.axis_index("lat")
 
     barrier = pltpu.get_barrier_semaphore()
+    pair = jnp.bitwise_xor(lat, 1)
+    north, south = ring(lat + 1), ring(lat + BANDS - 1)
+    other = north + south - pair
     for d in FAR:
-        pl.semaphore_signal(barrier, inc=1, device_id={"lon": ring(me + d)}, device_id_type=MESH)
-    north, south = ring(lat + 1), ring(lat + BANDS - 1)
-    for peer in (north, south):
-        pl.semaphore_signal(barrier, inc=1, device_id={"lat": peer}, device_id_type=MESH)
+        pl.semaphore_signal(barrier, inc=1, device_id={"lon": ring(me + d), "lat": pair}, device_id_type=MESH)
+    pl.semaphore_signal(barrier, inc=1, device_id={"lat": other}, device_id_type=MESH)
+    pl.semaphore_signal(barrier, inc=1, device_id={"lon": ring(me + RING - 1)}, device_id_type=MESH)
 
     def of_home(h, part):
         rows = pl.ds(pl.multiple_of(HALF + (h % 2) * HALF, HALF), HALF)
         return qx.at[pl.ds(part * EACH, EACH), h // 2, rows, :]
 
     own_q = pltpu.make_async_copy(q_hbm, qx.at[:, :, pl.ds(8, ROWS), :], sl.at[0])
-    own_s = pltpu.make_async_copy(s_hbm, s_ref, sl.at[1])
     own_c = pltpu.make_async_copy(c_hbm, cv, sl.at[2])
     own_v = pltpu.make_async_copy(v_hbm, mx.at[:, pl.ds(8, ROWS), :], sl.at[3])
-    for copy in (own_q, own_s, own_c, own_v):
+    for copy in (own_q, own_c, own_v):
         copy.start()
+
+    lane8, row8 = lanes_iota(HALF), rows_iota(HALF)
+    own_c.wait()
+    packed = jnp.zeros((HALF, LON), jnp.float32)
+    for tile in range(2 * LEV):
+        column = cv[tile // 2, HALF * (tile % 2) : HALF * (tile % 2) + HALF, LON - 1 : LON]
+        packed = jnp.where(lane8 == HALF * tile + row8, column, packed)
+    cw_out[...] = jnp.broadcast_to(jnp.sum(packed, axis=0, keepdims=True), (HALF, LON))
+
     own_q.wait()
-    own = [pltpu.make_async_copy(of_home(me, p), gat.at[me, pl.ds(p * EACH, EACH)], sl.at[4 + p]) for p in range(PARTS)]
-    for copy in own:
+    pl.semaphore_wait(barrier, RING + 2)
+
+    def gather_copy(d, part):
+        target = ring(me + d)
+        return pltpu.make_async_remote_copy(
+            of_home(target, part), gat.at[part, me], s1.at[part], r1.at[part],
+            device_id={"lon": target, "lat": pair}, device_id_type=MESH,
+        )
+
+    for part in range(PARTS):
+        for d in FAR:
+            gather_copy(d, part).start()
+
+    steps = pltpu.make_async_remote_copy(
+        s_hbm, s_ref, se.at[1], re.at[1], device_id={"lat": pair}, device_id_type=MESH
+    )
+    steps.start()
+
+    halo = [
+        (q_hbm.at[:, :, pl.ds(ROWS - 2, 2), :], qx.at[:, :, pl.ds(6, 2), :], north),
+        (q_hbm.at[:, :, pl.ds(0, 2), :], qx.at[:, :, pl.ds(24, 2), :], south),
+        (v_hbm.at[:, pl.ds(ROWS - 1, 1), :], mx.at[:, pl.ds(7, 1), :], north),
+    ]
+    halo = [
+        pltpu.make_async_remote_copy(a, b, sh.at[i], rh.at[i], device_id={"lat": p}, device_id_type=MESH)
+        for i, (a, b, p) in enumerate(halo)
+    ]
+    for copy in halo:
         copy.start()
-
-    lane8, row8 = lanes_iota(HALF), rows_iota(HALF)
-    own_s.wait()
+    edge = pltpu.make_async_remote_copy(
+        cw_out, cw_in, se.at[0], re.at[0], device_id={"lon": ring(me + 1)}, device_id_type=MESH
+    )
+    edge.start()
+
+    steps.wait_recv()
     line = s_ref[pl.ds(me // 2, 1), :].astype(jnp.float32)
     pick = lax.broadcasted_iota(jnp.int32, (HALF, ROWS), 1) == (
         lax.broadcasted_iota(jnp.int32, (HALF, ROWS), 0) + HALF * (me % 2)
@@ -90,42 +129,6 @@
     group = lane8 // WIDE
     ends = jnp.where(group == 0, LON - 1, jnp.where(group == 1, 0, 1))
 
-    own_c.wait()
-    packed = jnp.zeros((HALF, LON), jnp.float32)
-    for tile in range(2 * LEV):
-        column = cv[tile // 2, HALF * (tile % 2) : HALF * (tile % 2) + HALF, LON - 1 : LON]
-        packed = jnp.where(lane8 == HALF * tile + row8, column, packed)
-    cw_out[...] = jnp.broadcast_to(jnp.sum(packed, axis=0, keepdims=True), (HALF, LON))
-
-    pl.semaphore_wait(barrier, RING + 1)
-
-    def gather_copy(d, part):
-        target = ring(me + d)
-        return pltpu.make_async_remote_copy(
-            of_home(target, part), gat.at[me, pl.ds(part * EACH, EACH)], s1.at[part, d], r1.at[part, d],
-            device_id={"lon": target}, device_id_type=MESH,
-        )
-
-    for part in range(PARTS):
-        for d in FAR:
-            gather_copy(d, part).start()
-
-    halo = [
-        (q_hbm.at[:, :, pl.ds(ROWS - 2, 2), :], qx.at[:, :, pl.ds(6, 2), :], north),
-        (q_hbm.at[:, :, pl.ds(0, 2), :], qx.at[:, :, pl.ds(24, 2), :], south),
-        (v_hbm.at[:, pl.ds(ROWS - 1, 1), :], mx.at[:, pl.ds(7, 1), :], north),
-    ]
-    halo = [
-        pltpu.make_async_remote_copy(a, b, sh.at[i], rh.at[i], device_id={"lat": p}, device_id_type=MESH)
-        for i, (a, b, p) in enumerate(halo)
-    ]
-    for copy in halo:
-        copy.start()
-    edge = pltpu.make_async_remote_copy(
-        cw_out, cw_in, se.at[0], re.at[0], device_id={"lon": ring(me + 1)}, device_id_type=MESH
-    )
-    edge.start()
-
     own_v.wait()
     for copy in halo:
         copy.wait_recv()
@@ -154,21 +157,24 @@
 
     lax.fori_loop(0, LEV, meridional, 0)
 
+    def away(t):
+        hops = jnp.bitwise_and(t - me + RING, 7)
+        hops = jnp.minimum(hops, 8 - hops)
+        return jnp.where(hops == 0, 3, hops - 1)
+
     def return_copy(t, part):
         return pltpu.make_async_remote_copy(
-            ret.at[part, t, pl.ds(0, SIZE)], back.at[part, me, pl.ds(0, SIZE)], s2.at[part, t], r2.at[part, me],
-            device_id={"lon": t}, device_id_type=MESH,
+            ret.at[part, t, pl.ds(0, SIZE)], back.at[part, me, pl.ds(0, SIZE)], s2.at[part], r2.at[part, away(t)],
+            device_id={"lon": t, "lat": pair}, device_id_type=MESH,
         )
 
+    def take_bytes(ref, sem):
+        pltpu.make_async_copy(ref, ref, sem).wait()
+
     for part in range(PARTS):
-        own[part].wait()
-        for d in FAR[::-1]:
-            gather_copy(d, part).wait_recv()
-
-        rows_of = []
+        take_bytes(gat.at[part], r1.at[part])
         for i in range(EACH):
-            tr = part * EACH + i
-            blocks = [gat[b, tr] for b in range(RING)]
+            blocks = [gat[part, b, i] for b in range(RING)]
             mine = ((lane8 // HALF) % EACH == i) & (lane8 % HALF == row8)
             one = [jnp.where(bits[0], blocks[(b - 2) % RING], blocks[(b - 3) % RING]) for b in range(RING)]
             two = [jnp.where(bits[1], one[(b + 2) % RING], one[b]) for b in range(RING)]
@@ -189,13 +195,7 @@
             ret[part, b, WIDE:SIZE, :] = jnp.sum(pack[b], axis=0, keepdims=True)
 
         for t in ORDER:
-            @pl.when(t != me)
-            def _():
-                return_copy(t, part).start()
-
-        pltpu.make_async_copy(
-            ret.at[part, me, pl.ds(0, SIZE)], back.at[part, me, pl.ds(0, SIZE)], r2.at[part, me]
-        ).start()
+            return_copy(t, part).start()
 
     edge.wait_recv()
     west_row = jnp.broadcast_to(cw_in[0:1, :], (HALF, LON))
@@ -211,10 +211,7 @@
         past = jnp.where(d == 4, 4, 0)
         homes = [ring(me + d), ring(me + RING - d), ring(me + 8 + d + past), ring(me + 8 - d + past)]
         places = [(h // 2, pl.multiple_of((h % 2) * HALF, HALF)) for h in homes]
-        for h in homes:
-            pltpu.make_async_copy(
-                ret.at[part, h, pl.ds(0, SIZE)], back.at[part, h, pl.ds(0, SIZE)], r2.at[part, h]
-            ).wait()
+        take_bytes(back.at[part, pl.ds(0, 4), pl.ds(0, SIZE)], r2.at[part, d - 1])
         cells = jnp.concatenate([back[part, h, 0:WIDE] for h in homes], axis=0)
         extra = jnp.concatenate(
             [jnp.broadcast_to(back[part, h, WIDE:SIZE], (WIDE, LON)) for h in homes], axis=0
@@ -256,48 +253,31 @@
                 base[spot] = base[spot] - change[at : at + HALF]
                 at += HALF
 
-    written = []
     for part in range(PARTS):
         def step(d, carry):
             finish(part, d)
             return carry
 
         lax.fori_loop(1, 5, step, 0)
-        some = pl.ds(part * EACH, EACH)
-        for i, (src, dst) in enumerate(((flux_v, flux_hbm), (base, upd_hbm))):
-            copy = pltpu.make_async_copy(src.at[some], dst.at[some], so.at[part, i])
-            copy.start()
-            written.append(copy)
 
     for part in range(PARTS):
-        for d in FAR:
-            gather_copy(d, part).wait_send()
-        for t in ORDER:
-            @pl.when(t != me)
-            def _():
-                return_copy(t, part).wait_send()
+        take_bytes(gat.at[part], s1.at[part])
+        take_bytes(back.at[part, :, pl.ds(0, SIZE)], s2.at[part])
     for copy in halo:
         copy.wait_send()
     edge.wait_send()
-    for copy in written:
-        copy.wait()
-
-
-def hand_on(upd_in, flux_in, upd_out, flux_out, upd_v, flux_v, arrived, gone):
-    legs = []
-    for i, (src, mid, dst) in enumerate(((upd_in, upd_v, upd_out), (flux_in, flux_v, flux_out))):
-        for tr in range(TR):
-            legs.append((
-                pltpu.make_async_copy(src.at[tr], mid.at[tr], arrived.at[i, tr]),
-                pltpu.make_async_copy(mid.at[tr], dst.at[tr], gone.at[i, tr]),
-            ))
-    for first, _ in legs:
-        first.start()
-    for first, second in legs:
-        first.wait()
-        second.start()
-    for _, second in legs:
-        second.wait()
+    steps.wait_send()
+
+
+def hand_on(upd_in, flux_in, upd_out, flux_out, gone):
+    legs = [
+        pltpu.make_async_copy(src, dst, gone.at[i])
+        for i, (src, dst) in enumerate(((upd_in, upd_out), (flux_in, flux_out)))
+    ]
+    for leg in legs:
+        leg.start()
+    for leg in legs:
+        leg.wait()
 
 
 def per_device(tracers, courant_frac, shifts, merid):
@@ -305,39 +285,40 @@
     shape = jax.ShapeDtypeStruct((TR, LEV, ROWS, LON), f32)
     anywhere = pl.BlockSpec(memory_space=pl.ANY)
     tall = -(-SIZE // 8) * 8
+    held = pltpu.VMEM((TR, LEV, ROWS, LON), f32)
+    inside = pl.BlockSpec(memory_space=pltpu.VMEM)
+    inputs = [pltpu.with_memory_space_constraint(x, pltpu.HBM) for x in (tracers, courant_frac, shifts, merid)]
     updated, flux = pl.pallas_call(
         kernel,
-        out_shape=(shape, shape),
-        in_specs=[anywhere] * 4,
-        out_specs=(anywhere, anywhere),
+        out_shape=(held, held),
+        in_specs=[pl.BlockSpec(memory_space=pltpu.HBM)] * 4,
+        out_specs=(inside, inside),
         scratch_shapes=[
             vmem((LEV, ROWS), jnp.int32),
             vmem((TR, LEV, 32, LON), f32),
             vmem((LEV, 32, LON), f32),
             vmem((LEV, ROWS, LON), f32),
-            vmem((RING, TR, HALF, LON), f32),
+            vmem((PARTS, RING, EACH, HALF, LON), f32),
             vmem((PARTS, RING, tall, LON), f32),
             vmem((PARTS, RING, tall, LON), f32),
             vmem((RING, HALF, LON), f32),
-            vmem((TR, LEV, ROWS, LON), f32),
-            vmem((TR, LEV, ROWS, LON), f32),
             vmem((HALF, LON), f32),
             vmem((HALF, LON), f32),
-            dma((PARTS, RING)), dma((PARTS, RING)), dma((PARTS, RING)), dma((PARTS, RING)),
-            dma((4 + PARTS,)), dma((3,)), dma((3,)), dma((1,)), dma((1,)), dma((PARTS, 2)),
+            dma((PARTS,)), dma((PARTS,)), dma((PARTS,)), dma((PARTS, 4)),
+            dma((4,)), dma((3,)), dma((3,)), dma((2,)), dma((2,)),
         ],
-        compiler_params=pltpu.CompilerParams(collective_id=0, has_side_effects=True),
+        compiler_params=pltpu.CompilerParams(collective_id=0, has_side_effects=True, vmem_limit_bytes=16 * 2**20),
         cost_estimate=pl.CostEstimate(flops=100_000_000, bytes_accessed=1_000_000, transcendentals=0),
-    )(tracers, courant_frac, shifts, merid)
-    whole = vmem((TR, LEV, ROWS, LON), f32)
+    )(*inputs)
     return pl.pallas_call(
         hand_on,
         out_shape=(shape, shape),
-        in_specs=[anywhere] * 2,
+        in_specs=[inside] * 2,
         out_specs=(anywhere, anywhere),
-        scratch_shapes=[whole, whole, dma((2, TR)), dma((2, TR))],
-        cost_estimate=pl.CostEstimate(flops=0, bytes_accessed=2_000_000, transcendentals=0),
-    )(updated, flux)
+        scratch_shapes=[dma((2,))],
+        compiler_params=pltpu.CompilerParams(vmem_limit_bytes=2**20),
+        cost_estimate=pl.CostEstimate(flops=0, bytes_accessed=1_000_000, transcendentals=0),
+    )(*(pltpu.with_memory_space_constraint(x, pltpu.VMEM) for x in (updated, flux)))
 
 
 def solution(mesh):

time: 28.2 us -> 26.1 us (0.926)
  the two profiles are of different devices: /device:TPU:6 before, /device:TPU:1 now
where the time goes in v3:
time: 26.1 us; the launch traced here: 26 us
  Pallas kernels  25.4 us (97%)
  between operations  0.64 us (2%)
    pallas_call x1, Pallas kernels, per_device(): pl.pallas_call(kernel, out_shape=(held, held), in_specs=[pl.BlockSpec(mem...  24.6 us
    pallas_call x1, Pallas kernels, per_device(): pl.pallas_call(hand_on, out_shape=(shape, shape), in_specs=[inside] * 2,...  0.81 us

profile of v3, /device:TPU:1, one launch (start us, length us, event | category | flops | bytes accessed | tf_op | source)
XLA Modules:
  0.0 26.0 jit_solution(6537844402816310869)
XLA Ops:
  0.6 24.6 %shard_map.59 = (f32[4,8,16,128]{3,2,1,0:T(8,128)S(1)}, f32[4,8,16,128]{3,2,1,0:T(8,128)S(1)}) custom-call(f32[4,8,16,128]{3,2,1,0:T(8,128)} %q_hbm.1, f32[8,16,128]{2,1,0:T(8,128)} %c_hbm.1, s32[8,16]{1,0:T(8,128)} %s_hbm.1, f32[8,16,128]{2,1,0:T(8,128)} %v_hbm.1), custom_call_target="tpu_custom_call" | custom-call | flops 100000000 | bytes 1000000 | tf_op jit(solution)/shard_map/pallas_call | solution.py:291
  25.2 0.8 %shard_map.60 = (f32[4,8,16,128]{3,2,1,0:T(8,128)}, f32[4,8,16,128]{3,2,1,0:T(8,128)}) custom-call(f32[4,8,16,128]{3,2,1,0:T(8,128)S(1)} %get-tuple-element.4.upd_in, f32[4,8,16,128]{3,2,1,0:T(8,128)S(1)} %get-tuple-element.5.flux_in), custom_call_target="tpu_custom_call" | custom-call | bytes 1000000 | tf_op jit(solution)/shard_map/pallas_call | solution.py:313

commit v4 on v3

--- a/solution.py
+++ b/solution.py
@@ -15,8 +15,9 @@
 EACH = TR // PARTS
 WIDE = EACH * HALF
 SIZE = WIDE + 1
+FIN = PARTS // 2
 MESH = pl.DeviceIdType.MESH
-FAR = tuple(sorted(range(RING), key=lambda d: (-min(d % 8, 8 - d % 8), d)))
+FAR = tuple(sorted(range(1, RING), key=lambda d: (-min(d % 8, 8 - d % 8), d)))
 ORDER = (0, 8, 9, 1, 2, 10, 3, 11, 7, 15, 6, 14, 4, 12, 5, 13)
 
 
@@ -45,22 +46,20 @@
     lat = lax.axis_index("lat")
 
     barrier = pltpu.get_barrier_semaphore()
-    pair = jnp.bitwise_xor(lat, 1)
     north, south = ring(lat + 1), ring(lat + BANDS - 1)
-    other = north + south - pair
     for d in FAR:
-        pl.semaphore_signal(barrier, inc=1, device_id={"lon": ring(me + d), "lat": pair}, device_id_type=MESH)
-    pl.semaphore_signal(barrier, inc=1, device_id={"lat": other}, device_id_type=MESH)
-    pl.semaphore_signal(barrier, inc=1, device_id={"lon": ring(me + RING - 1)}, device_id_type=MESH)
-
-    def of_home(h, part):
-        rows = pl.ds(pl.multiple_of(HALF + (h % 2) * HALF, HALF), HALF)
-        return qx.at[pl.ds(part * EACH, EACH), h // 2, rows, :]
+        pl.semaphore_signal(barrier, inc=1, device_id={"lon": ring(me + d)}, device_id_type=MESH)
+    for peer in (north, south):
+        pl.semaphore_signal(barrier, inc=1, device_id={"lat": peer}, device_id_type=MESH)
+
+    def of_home(h, tr):
+        return qx.at[tr, h // 2, pl.ds(pl.multiple_of(HALF + (h % 2) * HALF, HALF), HALF), :]
 
     own_q = pltpu.make_async_copy(q_hbm, qx.at[:, :, pl.ds(8, ROWS), :], sl.at[0])
     own_c = pltpu.make_async_copy(c_hbm, cv, sl.at[2])
     own_v = pltpu.make_async_copy(v_hbm, mx.at[:, pl.ds(8, ROWS), :], sl.at[3])
-    for copy in (own_q, own_c, own_v):
+    own_s = pltpu.make_async_copy(s_hbm, s_ref, sl.at[1])
+    for copy in (own_q, own_s, own_c, own_v):
         copy.start()
 
     lane8, row8 = lanes_iota(HALF), rows_iota(HALF)
@@ -72,23 +71,19 @@
     cw_out[...] = jnp.broadcast_to(jnp.sum(packed, axis=0, keepdims=True), (HALF, LON))
 
     own_q.wait()
-    pl.semaphore_wait(barrier, RING + 2)
-
-    def gather_copy(d, part):
+    pl.semaphore_wait(barrier, RING + 1)
+
+    def gather_copy(d, tr):
         target = ring(me + d)
         return pltpu.make_async_remote_copy(
-            of_home(target, part), gat.at[part, me], s1.at[part], r1.at[part],
-            device_id={"lon": target, "lat": pair}, device_id_type=MESH,
+            of_home(target, tr), gat.at[tr, me], s1.at[tr], r1.at[tr],
+            device_id={"lon": target}, device_id_type=MESH,
         )
 
-    for part in range(PARTS):
+    for tr in range(TR):
         for d in FAR:
-            gather_copy(d, part).start()
-
-    steps = pltpu.make_async_remote_copy(
-        s_hbm, s_ref, se.at[1], re.at[1], device_id={"lat": pair}, device_id_type=MESH
-    )
-    steps.start()
+            gather_copy(d, tr).start()
+        pltpu.make_async_copy(of_home(me, tr), gat.at[tr, me], r1.at[tr]).start()
 
     halo = [
         (q_hbm.at[:, :, pl.ds(ROWS - 2, 2), :], qx.at[:, :, pl.ds(6, 2), :], north),
@@ -106,7 +101,7 @@
     )
     edge.start()
 
-    steps.wait_recv()
+    own_s.wait()
     line = s_ref[pl.ds(me // 2, 1), :].astype(jnp.float32)
     pick = lax.broadcasted_iota(jnp.int32, (HALF, ROWS), 1) == (
         lax.broadcasted_iota(jnp.int32, (HALF, ROWS), 0) + HALF * (me % 2)
@@ -129,6 +124,56 @@
     group = lane8 // WIDE
     ends = jnp.where(group == 0, LON - 1, jnp.where(group == 1, 0, 1))
 
+    def away(t):
+        hops = jnp.bitwise_and(t - me + RING, 7)
+        hops = jnp.minimum(hops, 8 - hops)
+        return jnp.where(hops == 0, 3, hops - 1)
+
+    def return_copy(t, part, rows):
+        return pltpu.make_async_remote_copy(
+            ret.at[part, t, rows], back.at[part, me, rows], s2.at[part], r2.at[part, away(t)],
+            device_id={"lon": t}, device_id_type=MESH,
+        )
+
+    def send_back(part, rows):
+        for t in ORDER:
+            @pl.when(t != me)
+            def _():
+                return_copy(t, part, rows).start()
+
+        pltpu.make_async_copy(ret.at[part, me, rows], back.at[part, me, rows], r2.at[part, away(me)]).start()
+
+    def take_bytes(ref, sem):
+        pltpu.make_async_copy(ref, ref, sem).wait()
+
+    for part in range(PARTS):
+        for i in range(EACH):
+            tr = part * EACH + i
+            take_bytes(gat.at[tr], r1.at[tr])
+            blocks = [gat[tr, b] for b in range(RING)]
+            mine = ((lane8 // HALF) % EACH == i) & (lane8 % HALF == row8)
+            one = [jnp.where(bits[0], blocks[(b - 2) % RING], blocks[(b - 3) % RING]) for b in range(RING)]
+            two = [jnp.where(bits[1], one[(b + 2) % RING], one[b]) for b in range(RING)]
+            aligned = [take(jnp.where(bits[2], two[(b + 4) % RING], two[b]), turn) for b in range(RING)]
+            tips = [take(a, ends) for a in aligned]
+            for b in range(RING):
+                ret[part, b, HALF * i : HALF * i + HALF, :] = aligned[b]
+                total = blocks[(b - REACH) % RING] * signs[0]
+                for n in range(1, 2 * REACH):
+                    total = total + blocks[(b - REACH + n) % RING] * signs[n]
+                offset = jnp.sum(total, axis=1, keepdims=True)
+                extra = jnp.where(group == 0, tips[b - 1], jnp.where(group == 3, offset, tips[(b + 1) % RING]))
+                if i == 0:
+                    pack[b] = jnp.where(mine, extra, 0.0)
+                else:
+                    pack[b] = jnp.where(mine, extra, pack[b])
+            if i < EACH - 1:
+                send_back(part, pl.ds(HALF * i, HALF))
+        for b in range(RING):
+            ret[part, b, WIDE:SIZE, :] = jnp.sum(pack[b], axis=0, keepdims=True)
+
+        send_back(part, pl.ds(WIDE - HALF, HALF + 1))
+
     own_v.wait()
     for copy in halo:
         copy.wait_recv()
@@ -157,70 +202,32 @@
 
     lax.fori_loop(0, LEV, meridional, 0)
 
-    def away(t):
-        hops = jnp.bitwise_and(t - me + RING, 7)
-        hops = jnp.minimum(hops, 8 - hops)
-        return jnp.where(hops == 0, 3, hops - 1)
-
-    def return_copy(t, part):
-        return pltpu.make_async_remote_copy(
-            ret.at[part, t, pl.ds(0, SIZE)], back.at[part, me, pl.ds(0, SIZE)], s2.at[part], r2.at[part, away(t)],
-            device_id={"lon": t, "lat": pair}, device_id_type=MESH,
-        )
-
-    def take_bytes(ref, sem):
-        pltpu.make_async_copy(ref, ref, sem).wait()
-
-    for part in range(PARTS):
-        take_bytes(gat.at[part], r1.at[part])
-        for i in range(EACH):
-            blocks = [gat[part, b, i] for b in range(RING)]
-            mine = ((lane8 // HALF) % EACH == i) & (lane8 % HALF == row8)
-            one = [jnp.where(bits[0], blocks[(b - 2) % RING], blocks[(b - 3) % RING]) for b in range(RING)]
-            two = [jnp.where(bits[1], one[(b + 2) % RING], one[b]) for b in range(RING)]
-            aligned = [take(jnp.where(bits[2], two[(b + 4) % RING], two[b]), turn) for b in range(RING)]
-            tips = [take(a, ends) for a in aligned]
-            for b in range(RING):
-                ret[part, b, HALF * i : HALF * i + HALF, :] = aligned[b]
-                total = blocks[(b - REACH) % RING] * signs[0]
-                for n in range(1, 2 * REACH):
-                    total = total + blocks[(b - REACH + n) % RING] * signs[n]
-                offset = jnp.sum(total, axis=1, keepdims=True)
-                extra = jnp.where(group == 0, tips[b - 1], jnp.where(group == 3, offset, tips[(b + 1) % RING]))
-                if i == 0:
-                    pack[b] = jnp.where(mine, extra, 0.0)
-                else:
-                    pack[b] = jnp.where(mine, extra, pack[b])
-        for b in range(RING):
-            ret[part, b, WIDE:SIZE, :] = jnp.sum(pack[b], axis=0, keepdims=True)
-
-        for t in ORDER:
-            return_copy(t, part).start()
-
     edge.wait_recv()
     west_row = jnp.broadcast_to(cw_in[0:1, :], (HALF, LON))
     upper = jnp.where(
         lax.broadcasted_iota(jnp.int32, (LON, LON), 0) <= lax.broadcasted_iota(jnp.int32, (LON, LON), 1), 1.0, 0.0
     ).astype(jnp.bfloat16)
-    rows = 4 * WIDE
+    rows = 4 * FIN * WIDE
     lane, row = lanes_iota(rows), rows_iota(rows) % WIDE
     index_a = jnp.where(lane == LON - 2, 1, jnp.where(lane == LON - 1, 2, 0)) * WIDE + row
     index_b = jnp.where(lane == LON - 1, 1, 3) * WIDE + row
 
-    def finish(part, d):
+    def finish(parts, d):
         past = jnp.where(d == 4, 4, 0)
         homes = [ring(me + d), ring(me + RING - d), ring(me + 8 + d + past), ring(me + 8 - d + past)]
         places = [(h // 2, pl.multiple_of((h % 2) * HALF, HALF)) for h in homes]
-        take_bytes(back.at[part, pl.ds(0, 4), pl.ds(0, SIZE)], r2.at[part, d - 1])
-        cells = jnp.concatenate([back[part, h, 0:WIDE] for h in homes], axis=0)
+        for part in parts:
+            take_bytes(back.at[part, pl.ds(0, 4), pl.ds(0, SIZE)], r2.at[part, d - 1])
+        cells = jnp.concatenate([back[part, h, 0:WIDE] for h in homes for part in parts], axis=0)
         extra = jnp.concatenate(
-            [jnp.broadcast_to(back[part, h, WIDE:SIZE], (WIDE, LON)) for h in homes], axis=0
+            [jnp.broadcast_to(back[part, h, WIDE:SIZE], (WIDE, LON)) for h in homes for part in parts], axis=0
         )
         ext_a, ext_b = take(extra, index_a), take(extra, index_b)
         plus1 = jnp.where(lane == LON - 1, ext_b, pltpu.roll(cells, LON - 1, 1))
         plus2 = jnp.where(lane >= LON - 2, ext_a, pltpu.roll(cells, LON - 2, 1))
+        tracers = range(parts[0] * EACH, (parts[-1] + 1) * EACH)
         q = jnp.concatenate(
-            [qx[part * EACH + i, l, pl.ds(start + 8, HALF), :] for l, start in places for i in range(EACH)], axis=0
+            [qx[tr, l, pl.ds(start + 8, HALF), :] for l, start in places for tr in tracers], axis=0
         )
         diff = q - cells
         part0 = diff.astype(jnp.bfloat16)
@@ -238,7 +245,7 @@
             t = [1.0 - x for x in c]
             tt = [(x * x - x) * 0.25 for x in t]
             for w in (t, tt):
-                weights.append(jnp.concatenate([x for x in w for _ in range(EACH)], axis=0))
+                weights.append(jnp.concatenate([x for x in w for _ in tracers], axis=0))
         t, tt, t_west, tt_west = weights
         offset = jnp.broadcast_to(ext_b[:, 0:1], (rows, LON))
         flux = sums - offset - (plus1 * t + (plus2 - cells) * tt)
@@ -247,26 +254,26 @@
         change = flux - flux_west
         at = 0
         for l, start in places:
-            for i in range(EACH):
-                spot = (part * EACH + i, l, pl.ds(start, HALF), slice(None))
+            for tr in tracers:
+                spot = (tr, l, pl.ds(start, HALF), slice(None))
                 flux_v[spot] = flux[at : at + HALF]
                 base[spot] = base[spot] - change[at : at + HALF]
                 at += HALF
 
+    for first_part in range(0, PARTS, FIN):
+        def step(d, carry):
+            finish(range(first_part, first_part + FIN), d)
+            return carry
+
+        lax.fori_loop(1, 5, step, 0)
+
     for part in range(PARTS):
-        def step(d, carry):
-            finish(part, d)
-            return carry
-
-        lax.fori_loop(1, 5, step, 0)
-
-    for part in range(PARTS):
-        take_bytes(gat.at[part], s1.at[part])
-        take_bytes(back.at[part, :, pl.ds(0, SIZE)], s2.at[part])
+        take_bytes(back.at[part, pl.ds(0, RING - 1), pl.ds(0, SIZE)], s2.at[part])
+    for tr in range(TR):
+        take_bytes(gat.at[tr, pl.ds(0, RING - 1)], s1.at[tr])
     for copy in halo:
         copy.wait_send()
     edge.wait_send()
-    steps.wait_send()
 
 
 def hand_on(upd_in, flux_in, upd_out, flux_out, gone):
@@ -298,14 +305,14 @@
             vmem((TR, LEV, 32, LON), f32),
             vmem((LEV, 32, LON), f32),
             vmem((LEV, ROWS, LON), f32),
-            vmem((PARTS, RING, EACH, HALF, LON), f32),
+            vmem((TR, RING, HALF, LON), f32),
             vmem((PARTS, RING, tall, LON), f32),
             vmem((PARTS, RING, tall, LON), f32),
             vmem((RING, HALF, LON), f32),
             vmem((HALF, LON), f32),
             vmem((HALF, LON), f32),
-            dma((PARTS,)), dma((PARTS,)), dma((PARTS,)), dma((PARTS, 4)),
-            dma((4,)), dma((3,)), dma((3,)), dma((2,)), dma((2,)),
+            dma((TR,)), dma((TR,)), dma((PARTS,)), dma((PARTS, 4)),
+            dma((4,)), dma((3,)), dma((3,)), dma((1,)), dma((1,)),
         ],
         compiler_params=pltpu.CompilerParams(collective_id=0, has_side_effects=True, vmem_limit_bytes=16 * 2**20),
         cost_estimate=pl.CostEstimate(flops=100_000_000, bytes_accessed=1_000_000, transcendentals=0),

time: 26.1 us -> 25.1 us (0.962)
  the two profiles are of different devices: /device:TPU:1 before, /device:TPU:6 now
where the time goes in v4:
time: 25.1 us; the launch traced here: 25 us
  Pallas kernels  24.4 us (97%)
  between operations  0.64 us (3%)
    pallas_call x1, Pallas kernels, per_device(): pl.pallas_call(kernel, out_shape=(held, held), in_specs=[pl.BlockSpec(mem...  23.6 us
    pallas_call x1, Pallas kernels, per_device(): pl.pallas_call(hand_on, out_shape=(shape, shape), in_specs=[inside] * 2,...  0.81 us

profile of v4, /device:TPU:6, one launch (start us, length us, event | category | flops | bytes accessed | tf_op | source)
XLA Modules:
  0.0 25.0 jit_solution(7425576258007857086)
XLA Ops:
  0.6 23.6 %shard_map.59 = (f32[4,8,16,128]{3,2,1,0:T(8,128)S(1)}, f32[4,8,16,128]{3,2,1,0:T(8,128)S(1)}) custom-call(f32[4,8,16,128]{3,2,1,0:T(8,128)} %q_hbm.1, f32[8,16,128]{2,1,0:T(8,128)} %c_hbm.1, s32[8,16]{1,0:T(8,128)} %s_hbm.1, f32[8,16,128]{2,1,0:T(8,128)} %v_hbm.1), custom_call_target="tpu_custom_call" | custom-call | flops 100000000 | bytes 1000000 | tf_op jit(solution)/shard_map/pallas_call | solution.py:298
  24.2 0.8 %shard_map.60 = (f32[4,8,16,128]{3,2,1,0:T(8,128)}, f32[4,8,16,128]{3,2,1,0:T(8,128)}) custom-call(f32[4,8,16,128]{3,2,1,0:T(8,128)S(1)} %get-tuple-element.4.upd_in, f32[4,8,16,128]{3,2,1,0:T(8,128)S(1)} %get-tuple-element.5.flux_in), custom_call_target="tpu_custom_call" | custom-call | bytes 1000000 | tf_op jit(solution)/shard_map/pallas_call | solution.py:320

commit v5 on v4

--- a/solution.py
+++ b/solution.py
@@ -40,62 +40,65 @@
 def kernel(
     q_hbm, c_hbm, s_hbm, v_hbm, base, flux_v,
     s_ref, qx, mx, cv, gat, ret, back, pack, cw_out, cw_in,
-    s1, r1, s2, r2, sl, sh, rh, se, re,
+    s1, r1, s2, r2, sl, sh, rh, se, re, ready,
 ):
     me = lax.axis_index("lon")
     lat = lax.axis_index("lat")
+
+    own_q = pltpu.make_async_copy(q_hbm, qx.at[:, :, pl.ds(8, ROWS), :], sl.at[0])
+    own_c = pltpu.make_async_copy(c_hbm, cv, sl.at[2])
+    own_v = pltpu.make_async_copy(v_hbm, mx.at[:, pl.ds(8, ROWS), :], sl.at[3])
+    own_s = pltpu.make_async_copy(s_hbm, s_ref, sl.at[1])
+    own_q.start()
 
     barrier = pltpu.get_barrier_semaphore()
     north, south = ring(lat + 1), ring(lat + BANDS - 1)
     for d in FAR:
         pl.semaphore_signal(barrier, inc=1, device_id={"lon": ring(me + d)}, device_id_type=MESH)
-    for peer in (north, south):
-        pl.semaphore_signal(barrier, inc=1, device_id={"lat": peer}, device_id_type=MESH)
+    pl.semaphore_signal(barrier, inc=1, device_id={"lat": south}, device_id_type=MESH)
 
     def of_home(h, tr):
         return qx.at[tr, h // 2, pl.ds(pl.multiple_of(HALF + (h % 2) * HALF, HALF), HALF), :]
 
-    own_q = pltpu.make_async_copy(q_hbm, qx.at[:, :, pl.ds(8, ROWS), :], sl.at[0])
-    own_c = pltpu.make_async_copy(c_hbm, cv, sl.at[2])
-    own_v = pltpu.make_async_copy(v_hbm, mx.at[:, pl.ds(8, ROWS), :], sl.at[3])
-    own_s = pltpu.make_async_copy(s_hbm, s_ref, sl.at[1])
-    for copy in (own_q, own_s, own_c, own_v):
+    for copy in (own_s, own_c, own_v):
         copy.start()
 
     lane8, row8 = lanes_iota(HALF), rows_iota(HALF)
+    own_q.wait()
+    pl.semaphore_wait(barrier, RING)
+
+    def gather_copy(d, tr):
+        target = ring(me + d)
+        return pltpu.make_async_remote_copy(
+            of_home(target, tr), gat.at[tr, me], s1.at[tr], r1.at[tr],
+            device_id={"lon": target}, device_id_type=MESH,
+        )
+
+    for tr in range(TR):
+        for d in FAR:
+            gather_copy(d, tr).start()
+
+    for tr in range(TR):
+        pltpu.make_async_copy(of_home(me, tr), gat.at[tr, me], r1.at[tr]).start()
+
+    halo = [
+        (qx.at[:, :, pl.ds(8 + ROWS - 2, 2), :], qx.at[:, :, pl.ds(6, 2), :], north),
+        (qx.at[:, :, pl.ds(8, 2), :], qx.at[:, :, pl.ds(24, 2), :], south),
+        (v_hbm.at[:, pl.ds(ROWS - 1, 1), :], mx.at[:, pl.ds(7, 1), :], north),
+    ]
+    halo = [
+        pltpu.make_async_remote_copy(a, b, sh.at[i], rh.at[i], device_id={"lat": p}, device_id_type=MESH)
+        for i, (a, b, p) in enumerate(halo)
+    ]
+    pl.semaphore_signal(ready, inc=1, device_id={"lat": north}, device_id_type=MESH)
+    halo[0].start()
+    halo[2].start()
     own_c.wait()
     packed = jnp.zeros((HALF, LON), jnp.float32)
     for tile in range(2 * LEV):
         column = cv[tile // 2, HALF * (tile % 2) : HALF * (tile % 2) + HALF, LON - 1 : LON]
         packed = jnp.where(lane8 == HALF * tile + row8, column, packed)
     cw_out[...] = jnp.broadcast_to(jnp.sum(packed, axis=0, keepdims=True), (HALF, LON))
-
-    own_q.wait()
-    pl.semaphore_wait(barrier, RING + 1)
-
-    def gather_copy(d, tr):
-        target = ring(me + d)
-        return pltpu.make_async_remote_copy(
-            of_home(target, tr), gat.at[tr, me], s1.at[tr], r1.at[tr],
-            device_id={"lon": target}, device_id_type=MESH,
-        )
-
-    for tr in range(TR):
-        for d in FAR:
-            gather_copy(d, tr).start()
-        pltpu.make_async_copy(of_home(me, tr), gat.at[tr, me], r1.at[tr]).start()
-
-    halo = [
-        (q_hbm.at[:, :, pl.ds(ROWS - 2, 2), :], qx.at[:, :, pl.ds(6, 2), :], north),
-        (q_hbm.at[:, :, pl.ds(0, 2), :], qx.at[:, :, pl.ds(24, 2), :], south),
-        (v_hbm.at[:, pl.ds(ROWS - 1, 1), :], mx.at[:, pl.ds(7, 1), :], north),
-    ]
-    halo = [
-        pltpu.make_async_remote_copy(a, b, sh.at[i], rh.at[i], device_id={"lat": p}, device_id_type=MESH)
-        for i, (a, b, p) in enumerate(halo)
-    ]
-    for copy in halo:
-        copy.start()
     edge = pltpu.make_async_remote_copy(
         cw_out, cw_in, se.at[0], re.at[0], device_id={"lon": ring(me + 1)}, device_id_type=MESH
     )
@@ -124,6 +127,9 @@
     group = lane8 // WIDE
     ends = jnp.where(group == 0, LON - 1, jnp.where(group == 1, 0, 1))
 
+    pl.semaphore_wait(ready, 1)
+    halo[1].start()
+
     def away(t):
         hops = jnp.bitwise_and(t - me + RING, 7)
         hops = jnp.minimum(hops, 8 - hops)
@@ -155,9 +161,12 @@
             one = [jnp.where(bits[0], blocks[(b - 2) % RING], blocks[(b - 3) % RING]) for b in range(RING)]
             two = [jnp.where(bits[1], one[(b + 2) % RING], one[b]) for b in range(RING)]
             aligned = [take(jnp.where(bits[2], two[(b + 4) % RING], two[b]), turn) for b in range(RING)]
+            for b in range(RING):
+                ret[part, b, HALF * i : HALF * i + HALF, :] = aligned[b]
+            if i < EACH - 1:
+                send_back(part, pl.ds(HALF * i, HALF))
             tips = [take(a, ends) for a in aligned]
             for b in range(RING):
-                ret[part, b, HALF * i : HALF * i + HALF, :] = aligned[b]
                 total = blocks[(b - REACH) % RING] * signs[0]
                 for n in range(1, 2 * REACH):
                     total = total + blocks[(b - REACH + n) % RING] * signs[n]
@@ -167,8 +176,6 @@
                     pack[b] = jnp.where(mine, extra, 0.0)
                 else:
                     pack[b] = jnp.where(mine, extra, pack[b])
-            if i < EACH - 1:
-                send_back(part, pl.ds(HALF * i, HALF))
         for b in range(RING):
             ret[part, b, WIDE:SIZE, :] = jnp.sum(pack[b], axis=0, keepdims=True)
 
@@ -266,14 +273,16 @@
             return carry
 
         lax.fori_loop(1, 5, step, 0)
-
-    for part in range(PARTS):
-        take_bytes(back.at[part, pl.ds(0, RING - 1), pl.ds(0, SIZE)], s2.at[part])
-    for tr in range(TR):
-        take_bytes(gat.at[tr, pl.ds(0, RING - 1)], s1.at[tr])
-    for copy in halo:
-        copy.wait_send()
-    edge.wait_send()
+        if first_part == 0:
+            for part in range(PARTS - 1):
+                take_bytes(back.at[part, pl.ds(0, RING - 1), pl.ds(0, SIZE)], s2.at[part])
+            for tr in range(TR):
+                take_bytes(gat.at[tr, pl.ds(0, RING - 1)], s1.at[tr])
+            for copy in halo:
+                copy.wait_send()
+            edge.wait_send()
+
+    take_bytes(back.at[PARTS - 1, pl.ds(0, RING - 1), pl.ds(0, SIZE)], s2.at[PARTS - 1])
 
 
 def hand_on(upd_in, flux_in, upd_out, flux_out, gone):
@@ -313,6 +322,7 @@
             vmem((HALF, LON), f32),
             dma((TR,)), dma((TR,)), dma((PARTS,)), dma((PARTS, 4)),
             dma((4,)), dma((3,)), dma((3,)), dma((1,)), dma((1,)),
+            pltpu.SemaphoreType.REGULAR,
         ],
         compiler_params=pltpu.CompilerParams(collective_id=0, has_side_effects=True, vmem_limit_bytes=16 * 2**20),
         cost_estimate=pl.CostEstimate(flops=100_000_000, bytes_accessed=1_000_000, transcendentals=0),

time: 25.1 us -> 25 us (level)
  no operation moved by 1% of the time
where the time goes in v5:
time: 25 us; the launch traced here: 24.9 us
  Pallas kernels  24.3 us (97%)
  between operations  0.64 us (3%)
    pallas_call x1, Pallas kernels, per_device(): pl.pallas_call(kernel, out_shape=(held, held), in_specs=[pl.BlockSpec(mem...  23.5 us
    pallas_call x1, Pallas kernels, per_device(): pl.pallas_call(hand_on, out_shape=(shape, shape), in_specs=[inside] * 2,...  0.81 us

profile of v5, /device:TPU:6, one launch (start us, length us, event | category | flops | bytes accessed | tf_op | source)
XLA Modules:
  0.0 24.9 jit_solution(12235370775570270817)
XLA Ops:
  0.6 23.5 %shard_map.59 = (f32[4,8,16,128]{3,2,1,0:T(8,128)S(1)}, f32[4,8,16,128]{3,2,1,0:T(8,128)S(1)}) custom-call(f32[4,8,16,128]{3,2,1,0:T(8,128)} %q_hbm.1, f32[8,16,128]{2,1,0:T(8,128)} %c_hbm.1, s32[8,16]{1,0:T(8,128)} %s_hbm.1, f32[8,16,128]{2,1,0:T(8,128)} %v_hbm.1), custom_call_target="tpu_custom_call" | custom-call | flops 100000000 | bytes 1000000 | tf_op jit(solution)/shard_map/pallas_call | solution.py:307
  24.1 0.8 %shard_map.60 = (f32[4,8,16,128]{3,2,1,0:T(8,128)}, f32[4,8,16,128]{3,2,1,0:T(8,128)}) custom-call(f32[4,8,16,128]{3,2,1,0:T(8,128)S(1)} %get-tuple-element.4.upd_in, f32[4,8,16,128]{3,2,1,0:T(8,128)S(1)} %get-tuple-element.5.flux_in), custom_call_target="tpu_custom_call" | custom-call | bytes 1000000 | tf_op jit(solution)/shard_map/pallas_call | solution.py:330

commit v6 on v5

--- a/solution.py
+++ b/solution.py
@@ -11,11 +11,11 @@
 NLAT = ROWS * BANDS
 HALF = 8
 REACH = 3
-PARTS = 2
+PARTS = 1
 EACH = TR // PARTS
 WIDE = EACH * HALF
 SIZE = WIDE + 1
-FIN = PARTS // 2
+FIN = 1
 MESH = pl.DeviceIdType.MESH
 FAR = tuple(sorted(range(1, RING), key=lambda d: (-min(d % 8, 8 - d % 8), d)))
 ORDER = (0, 8, 9, 1, 2, 10, 3, 11, 7, 15, 6, 14, 4, 12, 5, 13)

time: 25 us -> 25 us (level)
  no operation moved by 1% of the time
where the time goes in v6:
time: 25 us; the launch traced here: 24.9 us
  Pallas kernels  24.3 us (97%)
  between operations  0.64 us (3%)
    pallas_call x1, Pallas kernels, per_device(): pl.pallas_call(kernel, out_shape=(held, held), in_specs=[pl.BlockSpec(mem...  23.5 us
    pallas_call x1, Pallas kernels, per_device(): pl.pallas_call(hand_on, out_shape=(shape, shape), in_specs=[inside] * 2,...  0.81 us

profile of v6, /device:TPU:6, one launch (start us, length us, event | category | flops | bytes accessed | tf_op | source)
XLA Modules:
  0.0 24.9 jit_solution(6599827937525141415)
XLA Ops:
  0.6 23.5 %shard_map.59 = (f32[4,8,16,128]{3,2,1,0:T(8,128)S(1)}, f32[4,8,16,128]{3,2,1,0:T(8,128)S(1)}) custom-call(f32[4,8,16,128]{3,2,1,0:T(8,128)} %q_hbm.1, f32[8,16,128]{2,1,0:T(8,128)} %c_hbm.1, s32[8,16]{1,0:T(8,128)} %s_hbm.1, f32[8,16,128]{2,1,0:T(8,128)} %v_hbm.1), custom_call_target="tpu_custom_call" | custom-call | flops 100000000 | bytes 1000000 | tf_op jit(solution)/shard_map/pallas_call | solution.py:307
  24.1 0.8 %shard_map.60 = (f32[4,8,16,128]{3,2,1,0:T(8,128)}, f32[4,8,16,128]{3,2,1,0:T(8,128)}) custom-call(f32[4,8,16,128]{3,2,1,0:T(8,128)S(1)} %get-tuple-element.4.upd_in, f32[4,8,16,128]{3,2,1,0:T(8,128)S(1)} %get-tuple-element.5.flux_in), custom_call_target="tpu_custom_call" | custom-call | bytes 1000000 | tf_op jit(solution)/shard_map/pallas_call | solution.py:330
